TPU v7x, 128 devices: a whole 4x4x4 slice. The times are simulated.
128 devices in a mesh: ctx: 32 (over z_lo, x, y), fsdp: 4 (over z_hi, core).
Axes of the slice: x: 4, y: 4, z: 4 (z_hi: 2, z_lo: 2; z = z_hi * 2 + z_lo), core: 2. Of those that a mesh axis runs over, the one named last changes fastest.
Arguments:
- inputs: bfloat16 [4, 4096, 1024], P('fsdp', 'ctx'), may hold values from -6 to 6
- cotangent: bfloat16 [4, 4096, 1024], P('fsdp', 'ctx'), may hold values from -6 to 6
- qkv_weight: bfloat16 [1024, 2048], P('fsdp'), may hold values from -0.1875 to 0.1875
- out_weight: bfloat16 [1024, 1024], P('fsdp'), may hold values from -1 to 1
- gate_weight: bfloat16 [1024, 4608], P('fsdp'), may hold values from -0.1875 to 0.1875
- up_weight: bfloat16 [1024, 4608], P('fsdp'), may hold values from -0.1875 to 0.1875
- down_weight: bfloat16 [4608, 1024], P('fsdp'), may hold values from -0.09375 to 0.09375
- gain_attn: float32 [1024], replicated, may hold values from 0.5 to 1.5
- gain_query: float32 [64], replicated, may hold values from 0.1 to 1.9
- gain_key: float32 [64], replicated, may hold values from 0.1 to 1.9
- gain_ffn: float32 [1024], replicated, may hold values from 0.5 to 1.5
- block_order: int32 [64], replicated, may hold values from 0 to 63, each once
- doc_starts: int32 [4, 4], P('fsdp'), may hold values from 0 to 4095, as said below
Outputs:
- outputs: bfloat16 [4, 4096, 1024], P('fsdp', 'ctx')
- grad_inputs: bfloat16 [4, 4096, 1024], P('fsdp', 'ctx')
- grad_qkv_weight: float32 [1024, 2048], P('fsdp')
- grad_out_weight: float32 [1024, 1024], P('fsdp')
- grad_gate_weight: float32 [1024, 4608], P('fsdp')
- grad_up_weight: float32 [1024, 4608], P('fsdp')
- grad_down_weight: float32 [4608, 1024], P('fsdp')
- grad_gain_attn: float32 [1024], replicated
- grad_gain_query: float32 [64], replicated
- grad_gain_key: float32 [64], replicated
- grad_gain_ffn: float32 [1024], replicated
Inputs may be any that keep to these rules, and one draw needn't show every extreme that they name: `doc_starts`: for each sequence, 4 strictly increasing document starts: the first is 0, the last is 4095, all others lie at or after 4096 - 4096 // 4.
All inputs are finite; a program needn't handle non-finite values.
Results may differ from a plain program's by a relative error of at most 0.03.
Values may be sent and summed in bfloat16 or wider, within the bound.
A program may use at most 256 MiB of HBM per device.

v0:
```python
import jax
import jax.numpy as jnp
from jax import lax
from jax.sharding import PartitionSpec as P

QUERY_HEADS = 16
KEY_VALUE_HEADS = 8
HEAD_SIZE = 64
FF = 4608


EPSILON = 1e-05
ROPE_BASE = 1000000.0
NEGATIVE_FILLER = -1e30


def side_by_side(arrays, axis, dim, along):
    ends, at = ([], 0)
    for a in arrays[:-1]:
        at += a.shape[along]
        ends.append(at)
    both = jnp.concatenate(arrays, axis=along)
    return tuple(jnp.split(lax.all_gather(both, axis, axis=dim, tiled=True), ends, axis=along))


def split_up(array, dim, peers):
    dims = array.shape
    pieces = array.reshape(*dims[:dim], peers, dims[dim] // peers, *dims[dim + 1 :])
    return jnp.moveaxis(pieces, dim, 0)


def summed_on_arrival(array, axis, dim):
    pieces = split_up(array, dim, lax.axis_size(axis))
    arrived = lax.all_to_all(pieces, axis, split_axis=0, concat_axis=0, tiled=True)
    return arrived.astype(jnp.float32).sum(axis=0)


def sum_packed(arrays, axis, dims):
    peers = lax.axis_size(axis)
    pieces = [split_up(a, dim, peers) for a, dim in zip(arrays, dims)]
    lines = jnp.concatenate([b.reshape(peers, -1) for b in pieces], axis=1)
    rows = max(16, -(-lines.shape[1] // 1024) * 8)
    lines = jnp.pad(lines, ((0, 0), (0, rows * 128 - lines.shape[1]))).reshape(-1, 128)
    ravelled, at, done = (lax.psum_scatter(lines, axis, tiled=True).reshape(-1), 0, [])
    for b in pieces:
        part = b[0]
        done.append(ravelled[at : at + part.size].reshape(part.shape))
        at += part.size
    return tuple(done)


def laid_out(pieces, dim):
    dims = list(pieces.shape[1:])
    dims[dim] *= pieces.shape[0]
    return jnp.moveaxis(pieces, 0, dim).reshape(dims)


def one_gather(arrays, axis, dims):
    ravelled = jnp.concatenate([a.reshape(-1) for a in arrays])
    lines, at, done = (lax.all_gather(ravelled, axis), 0, [])
    for a, dim in zip(arrays, dims):
        pieces = lines[:, at : at + a.size].reshape(-1, *a.shape)
        done.append(laid_out(pieces, dim))
        at += a.size
    return tuple(done)


def over_pieces(array, axis):
    pieces = lax.all_gather(array, axis)
    return pieces.sum(axis=0)


def rms_norm(values, gain_row):
    return (
        values * lax.rsqrt(jnp.mean(values * values, axis=-1, keepdims=True) + EPSILON) * gain_row
    )


def rotate(values, positions):
    half_width = values.shape[-1] // 2
    frequency = ROPE_BASE ** (-2.0 * jnp.arange(half_width, dtype=jnp.float32) / values.shape[-1])
    angles = positions.astype(jnp.float32)[:, None] * frequency[None, :]
    cosine = jnp.cos(angles)[:, None, :]
    sine_part = jnp.sin(angles)[:, None, :]
    first_half = values[..., :half_width]
    second_half = values[..., half_width:]
    return jnp.concatenate(
        [
            first_half * cosine - second_half * sine_part,
            second_half * cosine + first_half * sine_part,
        ],
        axis=-1,
    )


def outer_sum(left, right):
    return lax.dot_general(
        left, right, (((0,), (0,)), ((), ())), preferred_element_type=jnp.float32
    )


def positions_at(block_order, first_row, total_row_count, half_rows):
    row_ids = first_row + jnp.arange(total_row_count, dtype=jnp.int32)
    blocks = row_ids // half_rows
    lookup = jnp.arange(block_order.shape[0], dtype=jnp.int32)
    picked = jnp.sum(jnp.where(blocks[:, None] == lookup[None, :], block_order[None, :], 0), axis=1)
    return picked * half_rows + row_ids % half_rows


def segments_of(positions, starts_row):
    return jnp.sum((starts_row[None, :] <= positions[:, None]).astype(jnp.int32), axis=1) - 1


def score_block(query_four_axes, key_row_block, query_pos, query_seg, key_pos, key_seg):
    key_three_axes = key_row_block.reshape(key_row_block.shape[0], KEY_VALUE_HEADS, HEAD_SIZE)
    scores = jnp.einsum(
        "qhgd,khd->hgqk", query_four_axes, key_three_axes, preferred_element_type=jnp.float32
    ) * float(HEAD_SIZE) ** (-0.5)
    allowed = (key_pos[None, :] <= query_pos[:, None]) & (key_seg[None, :] == query_seg[:, None])
    return (scores, allowed)


def attend(
    softmax_stats,
    query_four_axes,
    key_row_block,
    value_row_block,
    query_pos,
    query_seg,
    key_pos,
    key_seg,
):
    row_max, row_sum, partial_value = softmax_stats
    scores, allowed = score_block(
        query_four_axes, key_row_block, query_pos, query_seg, key_pos, key_seg
    )
    scores = jnp.where(allowed, scores, NEGATIVE_FILLER)
    new_max = jnp.maximum(row_max, jnp.max(scores, axis=-1))
    prob_rows = jnp.where(allowed, jnp.exp(scores - new_max[..., None]), 0.0)
    row_sum = jnp.sum(prob_rows, axis=-1)
    value_three_axes = value_row_block.reshape(value_row_block.shape[0], KEY_VALUE_HEADS, HEAD_SIZE)
    update = jnp.einsum(
        "hgqk,khd->qhgd",
        prob_rows.astype(jnp.bfloat16),
        value_three_axes,
        preferred_element_type=jnp.float32,
    )
    partial_value = update
    return (new_max, row_sum, partial_value)


def attend_back(
    query_gradient,
    query_four_axes,
    gradient_four_axes,
    log_total,
    row_delta,
    key_row_block,
    value_row_block,
    query_pos,
    query_seg,
    key_pos,
    key_seg,
):
    total_row_count = key_row_block.shape[0]
    scores, allowed = score_block(
        query_four_axes, key_row_block, query_pos, query_seg, key_pos, key_seg
    )
    prob_rows = jnp.where(allowed, jnp.exp(scores - log_total[..., None]), 0.0)
    key_three_axes = key_row_block.reshape(total_row_count, KEY_VALUE_HEADS, HEAD_SIZE)
    value_three_axes = value_row_block.reshape(total_row_count, KEY_VALUE_HEADS, HEAD_SIZE)
    value_gradient = jnp.einsum(
        "hgqk,qhgd->khd",
        prob_rows.astype(jnp.bfloat16),
        gradient_four_axes,
        preferred_element_type=jnp.float32,
    )
    grad_prob = jnp.einsum(
        "qhgd,khd->hgqk", gradient_four_axes, value_three_axes, preferred_element_type=jnp.float32
    )
    grad_scores = (prob_rows * (grad_prob - row_delta[..., None])).astype(jnp.bfloat16)
    score_scale = float(HEAD_SIZE) ** (-0.5)
    query_gradient = (
        jnp.einsum(
            "hgqk,khd->qhgd", grad_scores, key_three_axes, preferred_element_type=jnp.float32
        )
        * score_scale
    )
    key_gradient = (
        jnp.einsum(
            "hgqk,qhgd->khd", grad_scores, query_four_axes, preferred_element_type=jnp.float32
        )
        * score_scale
    )
    return (
        query_gradient,
        key_gradient.reshape(total_row_count, KEY_VALUE_HEADS * HEAD_SIZE),
        value_gradient.reshape(total_row_count, KEY_VALUE_HEADS * HEAD_SIZE),
    )


def per_device(
    inputs,
    cotangent,
    qkv_weight,
    out_weight,
    gate_weight,
    up_weight,
    down_weight,
    gain_attn,
    gain_query,
    gain_key,
    gain_ffn,
    block_order,
    doc_starts,
):
    token_rows = inputs.shape[1]
    half_rows = token_rows // 2
    query_groups = QUERY_HEADS // KEY_VALUE_HEADS
    cycle_index = lax.axis_index("ctx")
    qkv_all, out_all, gate_all, up_all, down_all = (
        *side_by_side((qkv_weight, out_weight, gate_weight, up_weight), "fsdp", 0, 1),
        lax.all_gather(down_weight, "fsdp", axis=0, tiled=True),
    )
    starts_row = doc_starts[0]
    positions = positions_at(block_order, cycle_index * token_rows, token_rows, half_rows)
    segments = segments_of(positions, starts_row)

    def remote_keys(first_row, total_row_count):
        key_pos = positions_at(block_order, first_row, total_row_count, half_rows)
        return (key_pos, segments_of(key_pos, starts_row))

    resid_in = inputs[0].astype(jnp.float32)
    normed, norm_in_pull = jax.vjp(rms_norm, resid_in, gain_attn)
    normed_low = normed.astype(jnp.bfloat16)
    output_projection = jnp.dot(normed_low, qkv_all, preferred_element_type=jnp.float32)
    split_position = (QUERY_HEADS + KEY_VALUE_HEADS) * HEAD_SIZE

    def query_key(leading_columns, scale_query, scale_key):
        queries = leading_columns[:, : QUERY_HEADS * HEAD_SIZE].reshape(
            token_rows, QUERY_HEADS, HEAD_SIZE
        )
        unrotated_keys = leading_columns[:, QUERY_HEADS * HEAD_SIZE :].reshape(
            token_rows, KEY_VALUE_HEADS, HEAD_SIZE
        )
        return (
            rotate(rms_norm(queries, scale_query), positions),
            rotate(rms_norm(unrotated_keys, scale_key), positions),
        )

    (query_rotated, key_rotated), qk_pull = jax.vjp(
        query_key, output_projection[:, :split_position], gain_query, gain_key
    )
    query_four_axes = query_rotated.astype(jnp.bfloat16).reshape(
        token_rows, KEY_VALUE_HEADS, query_groups, HEAD_SIZE
    )
    key_row_block = key_rotated.astype(jnp.bfloat16).reshape(
        token_rows, KEY_VALUE_HEADS * HEAD_SIZE
    )
    value_row_block = output_projection[:, split_position:].astype(jnp.bfloat16)
    start_stats = (
        jnp.full((KEY_VALUE_HEADS, query_groups, token_rows), NEGATIVE_FILLER, jnp.float32),
        jnp.zeros((KEY_VALUE_HEADS, query_groups, token_rows), jnp.float32),
        jnp.zeros((token_rows, KEY_VALUE_HEADS, query_groups, HEAD_SIZE), jnp.float32),
    )
    kv_piece = side_by_side((key_row_block, value_row_block), "ctx", 0, 1)
    key_pos, key_seg = remote_keys(jnp.int32(0), kv_piece[0].shape[0])
    softmax_stats = attend(
        start_stats,
        query_four_axes,
        kv_piece[0],
        kv_piece[1],
        positions,
        segments,
        key_pos,
        key_seg,
    )
    row_max, row_sum, partial_value = softmax_stats
    log_total = row_max + jnp.log(row_sum)
    attention_output = (partial_value / jnp.transpose(row_sum, (2, 0, 1))[..., None]).reshape(
        token_rows, QUERY_HEADS * HEAD_SIZE
    )
    attended_low = attention_output.astype(jnp.bfloat16)
    residual = resid_in + jnp.dot(attended_low, out_all, preferred_element_type=jnp.float32)
    normed_ffn, norm_ffn_pull = jax.vjp(rms_norm, residual, gain_ffn)
    ffn_low = normed_ffn.astype(jnp.bfloat16)
    gate_proj = jnp.dot(ffn_low, gate_all, preferred_element_type=jnp.float32)
    up_proj = jnp.dot(ffn_low, up_all, preferred_element_type=jnp.float32)
    hidden, gating_pull = jax.vjp(
        lambda gate_in, up_in: jax.nn.silu(gate_in) * up_in, gate_proj, up_proj
    )
    hidden_low = hidden.astype(jnp.bfloat16)
    outputs = residual + jnp.dot(hidden_low, down_all, preferred_element_type=jnp.float32)
    grad_out = cotangent[0]
    grad_hidden = jnp.dot(grad_out, down_all.T, preferred_element_type=jnp.float32)
    down_part = lax.psum_scatter(
        outer_sum(hidden_low, grad_out).astype(jnp.bfloat16),
        "fsdp",
        scatter_dimension=0,
        tiled=True,
    )
    grad_gate, grad_up = gating_pull(grad_hidden)
    gate_low = grad_gate.astype(jnp.bfloat16)
    up_low = grad_up.astype(jnp.bfloat16)
    gate_up_part = lax.psum_scatter(
        jnp.concatenate([outer_sum(ffn_low, gate_low), outer_sum(ffn_low, up_low)], axis=1).astype(
            jnp.bfloat16
        ),
        "fsdp",
        scatter_dimension=0,
        tiled=True,
    )
    grad_ffn_in = jnp.dot(gate_low, gate_all.T, preferred_element_type=jnp.float32) + jnp.dot(
        up_low, up_all.T, preferred_element_type=jnp.float32
    )
    grad_resid_ffn, grad_gain_ffn = norm_ffn_pull(grad_ffn_in)
    grad_resid = grad_out.astype(jnp.float32) + grad_resid_ffn
    branch_low = grad_resid.astype(jnp.bfloat16)
    out_part = summed_on_arrival(
        outer_sum(attended_low, branch_low).astype(jnp.bfloat16), "fsdp", 0
    )
    attention_output_gradient = jnp.dot(
        branch_low, out_all.T, preferred_element_type=jnp.float32
    ).astype(jnp.bfloat16)
    gradient_four_axes = attention_output_gradient.reshape(
        token_rows, KEY_VALUE_HEADS, query_groups, HEAD_SIZE
    )
    row_delta = jnp.transpose(
        jnp.sum(
            gradient_four_axes.astype(jnp.float32)
            * attention_output.reshape(token_rows, KEY_VALUE_HEADS, query_groups, HEAD_SIZE),
            axis=-1,
        ),
        (1, 2, 0),
    )
    empty_query_gradient = jnp.zeros(
        (token_rows, KEY_VALUE_HEADS, query_groups, HEAD_SIZE), jnp.float32
    )
    kv_piece = side_by_side((key_row_block, value_row_block), "ctx", 0, 1)
    query_gradient = empty_query_gradient
    key_pos, key_seg = remote_keys(jnp.int32(0), kv_piece[0].shape[0])
    query_gradient, key_gradient, value_gradient = attend_back(
        query_gradient,
        query_four_axes,
        gradient_four_axes,
        log_total,
        row_delta,
        kv_piece[0],
        kv_piece[1],
        positions,
        segments,
        key_pos,
        key_seg,
    )
    gathered_grad = jnp.concatenate([key_gradient, value_gradient], axis=1)
    query_gradient, gathered_grad = (query_gradient, gathered_grad)
    summed_kv = lax.psum_scatter(
        gathered_grad.astype(jnp.bfloat16), "ctx", scatter_dimension=0, tiled=True
    ).astype(jnp.float32)
    key_gradient = summed_kv[:, : KEY_VALUE_HEADS * HEAD_SIZE]
    value_gradient = summed_kv[:, KEY_VALUE_HEADS * HEAD_SIZE :]
    grad_front, grad_gain_query, grad_gain_key = qk_pull(
        (
            query_gradient.reshape(token_rows, QUERY_HEADS, HEAD_SIZE),
            key_gradient.reshape(token_rows, KEY_VALUE_HEADS, HEAD_SIZE),
        )
    )
    grad_projected = jnp.concatenate([grad_front, value_gradient], axis=1).astype(jnp.bfloat16)
    qkv_part = lax.psum_scatter(
        outer_sum(normed_low, grad_projected).astype(jnp.bfloat16),
        "fsdp",
        scatter_dimension=0,
        tiled=True,
    )
    grad_normed = jnp.dot(grad_projected, qkv_all.T, preferred_element_type=jnp.float32)
    grad_input_norm, grad_gain_attn = norm_in_pull(grad_normed)
    grad_inputs = (grad_resid + grad_input_norm).astype(jnp.bfloat16)
    summed_parts = tuple(
        (
            part.astype(jnp.float32)
            for part in sum_packed(
                (qkv_part, out_part.astype(jnp.bfloat16), gate_up_part, down_part),
                "ctx",
                (1, 1, 1, 1),
            )
        )
    )
    shared_full = tuple(
        (
            part.astype(jnp.float32)
            for part in one_gather(
                (
                    summed_parts[0].astype(jnp.bfloat16),
                    summed_parts[1].astype(jnp.bfloat16),
                    summed_parts[2].astype(jnp.bfloat16),
                    summed_parts[3].astype(jnp.bfloat16),
                ),
                "ctx",
                (1, 1, 1, 1),
            )
        )
    )
    gain_sums = (
        over_pieces(grad_gain_attn, ("ctx", "fsdp")),
        over_pieces(grad_gain_query, ("ctx", "fsdp")),
        over_pieces(grad_gain_key, ("ctx", "fsdp")),
        over_pieces(grad_gain_ffn, ("ctx", "fsdp")),
    )
    return (
        outputs.astype(jnp.bfloat16)[None],
        grad_inputs[None],
        shared_full[0],
        shared_full[1],
        shared_full[2][:, :FF],
        shared_full[2][:, FF:],
        shared_full[3],
        gain_sums[0],
        gain_sums[1],
        gain_sums[2],
        gain_sums[3],
    )


def solution(mesh):
    in_specs = (
        P("fsdp", "ctx", None),
        P("fsdp", "ctx", None),
        P("fsdp", None),
        P("fsdp", None),
        P("fsdp", None),
        P("fsdp", None),
        P("fsdp", None),
        P(),
        P(),
        P(),
        P(),
        P(),
        P("fsdp", None),
    )
    out_specs = (
        P("fsdp", "ctx", None),
        P("fsdp", "ctx", None),
        P("fsdp", None),
        P("fsdp", None),
        P("fsdp", None),
        P("fsdp", None),
        P("fsdp", None),
        P(),
        P(),
        P(),
        P(),
    )
    return jax.shard_map(
        per_device, mesh=mesh, in_specs=in_specs, out_specs=out_specs, check_vma=False
    )
```

profile of v0, /device:TPU:0, one launch (start us, length us, event | category | flops | bytes accessed | tf_op | source)
XLA Modules:
  0.0 1792.0 jit_solution(5669525135201092699)
XLA Ops:
  15.4 159.9 %all-gather.10.cloned.1.call-done = bf16[1024,12288]{1,0:T(8,128)(2,1)} async-done(((bf16[256,12288]{1,0:T(8,128)(2,1)}), bf16[1024,12288]{1,0:T(8,128)(2,1)}) %all-gather.10.cloned.1.call-update) | async-done | bytes 25165840 | tf_op jit(solution)/shard_map/all_gather | solution.py:23
  182.0 62.6 %all-gather.14.cloned.1.call-done = bf16[4608,1024]{1,0:T(8,128)(2,1)} async-done(((bf16[1152,1024]{1,0:T(8,128)(2,1)}), bf16[4608,1024]{1,0:T(8,128)(2,1)}) %all-gather.14.cloned.1.call-update) | async-done | bytes 9437200 | tf_op jit(solution)/shard_map/all_gather | solution.py:223
  244.6 8.3 fusion.65
  253.5 159.7 %all-gather.12.cloned.1.call-done = bf16[4096,1024]{1,0:T(8,128)(2,1)} async-done(((bf16[128,1024]{1,0:T(8,128)(2,1)}), bf16[4096,1024]{1,0:T(8,128)(2,1)}) %all-gather.12.cloned.1.call-update) | async-done | bytes 8388624 | tf_op jit(solution)/shard_map/all_gather | solution.py:23
  425.3 15.1 fusion.4
  446.7 14.6 fusion.6
  462.0 17.2 fusion.99
  514.3 16.1 bitcast_convert_fusion
  530.4 22.9 %fusion.1 = bf16[8,2,128,4096]{2,3,1,0:T(8,128)(2,1)} fusion(f32[8,4096,128,2]{2,1,3,0:T(8,128)} %get-tuple-element.76, f32[8,2,128]{2,1,0:T(2,128)} %bitcast.196, f32[8,2,128]{2,1,0:T(2,128)} %log_add_fusion, pred[128,4096]{0,1:T(8,128)(4,1)S(1)} %compare_and_fusion, bf16[4096,8,64,1]{0,2,3,1:T(8,128)(2,1)} %bitcast.179, bf16[128,8,2,64]{0,3,2,1:T(8,128)(2,1)} %bitcast.189), kind=kOutput, calls=%fused_computation.2 | convolution fusion | flops 1124073472 | bytes 55328768 | tf_op jit(solution)/shard_map/qhgd,khd->hgqk/dot_general | solution.py:178
  553.3 10.1 fusion.14
  571.3 12.0 copy.127
  589.0 10.1 convolution_multiply_fusion
  600.9 162.8 %reduce-scatter.16.cloned.1.call-done = bf16[128,1024]{1,0:T(8,128)(2,1)} async-done(((bf16[4096,1024]{1,0:T(8,128)(2,1)}), bf16[128,1024]{1,0:T(8,128)(2,1)}) %reduce-scatter.16.cloned.1.call-update) | async-done | bytes 262160
  781.0 10.9 pad_maximum_fusion
  793.9 54.7 %all_to_all.5 = bf16[4,256,1024]{2,1,0:T(8,128)(2,1)} all-to-all(bf16[4,256,1024]{2,1,0:T(8,128)(2,1)S(1)} %bitcast.175), channel_id=1, replica_groups=mesh['ctx'=32,'fsdp'=4] {'fsdp'}, dimensions={0} | all-to-all | bytes 4194304 | tf_op jit(solution)/shard_map/all_to_all | solution.py:34
  858.0 13.0 reduce-scatter.12.cloned.1.call-done
  875.2 8.1 copy.109
  883.3 13.1 reshape.414
  896.4 28.1 %reduce-scatter.8.cloned.1.call-done = bf16[256,2048]{1,0:T(8,128)(2,1)} async-done(((bf16[1024,2048]{1,0:T(8,128)(2,1)}), bf16[256,2048]{1,0:T(8,128)(2,1)}) %reduce-scatter.8.cloned.1.call-update) | async-done | bytes 1048592 | tf_op jit(solution)/shard_map/reduce_scatter | solution.py:369
  933.2 140.0 %reduce-scatter.10.cloned.1.call-done = bf16[256,9216]{1,0:T(8,128)(2,1)} async-done(((bf16[1024,9216]{1,0:T(8,128)(2,1)}), bf16[256,9216]{1,0:T(8,128)(2,1)}) %reduce-scatter.10.cloned.1.call-update) | async-done | bytes 4718608 | tf_op jit(solution)/shard_map/reduce_scatter | solution.py:305
  1087.8 11.0 reshape.412
  1098.8 10.5 pad_maximum_fusion.1
  1109.3 9.3 reshape.415
  1120.3 177.6 %reduce-scatter.14.cloned.1.call-done = bf16[1056,128]{1,0:T(8,128)(2,1)} async-done(((bf16[33792,128]{1,0:T(8,128)(2,1)}), bf16[1056,128]{1,0:T(8,128)(2,1)}) %reduce-scatter.14.cloned.1.call-update) | async-done | bytes 270352 | tf_op jit(solution)/shard_map/reduce_scatter | solution.py:44
  1302.0 174.5 %all-gather.4 = f32[131072]{0:T(1024)S(1)} all-gather(f32[1024]{0:T(1024)S(1)} %copy-done.37), channel_id=6, replica_groups=mesh['ctx'=32,'fsdp'=4] {'ctx','fsdp'}, dimensions={0}, use_global_device_ids=true | all-gather | bytes 528384 | tf_op jit(solution)/shard_map/all_gather | solution.py:69
  1488.8 172.2 %all-gather.1 = f32[131072]{0:T(1024)S(1)} all-gather(f32[1024]{0:T(1024)S(1)} %get-tuple-element.46), channel_id=3, replica_groups=mesh['ctx'=32,'fsdp'=4] {'ctx','fsdp'}, dimensions={0}, use_global_device_ids=true | all-gather | bytes 528384 | tf_op jit(solution)/shard_map/all_gather | solution.py:69
  1665.4 9.1 reshape.433
  1702.1 12.7 reshape.431
  1714.9 11.5 copy.112
  1726.4 8.1 fusion.96
  1746.6 19.9 %reshape.432 = f32[32,1152,32]{2,1,0:T(8,128)} reshape(f32[32,36864]{1,0:T(8,128)} %slice_convert_fusion.1) | data formatting | bytes 9437184 | tf_op jit(solution)/shard_map/convert_element_type | solution.py:390
  1766.5 12.2 copy.113
  (221 shorter events, 208.7 us)
Async XLA Ops:
  7.2 168.0 %copy-start.24 = (f32[1024]{0:T(1024)S(1)}, f32[1024]{0:T(1024)}, u32[]{:S(2)}) copy-start(f32[1024]{0:T(1024)} %param.20) | copy-start | bytes 12292
  7.2 168.0 %all-gather.10.cloned.1.call-start = ((), (), s32[]{:S(2)}) async-start(), calls=%async_computation.6 | async-start | bytes 31457280 | tf_op jit(solution)/shard_map/all_gather | solution.py:23
  13.6 164.9 %copy-start.36 = (f32[64]{0:T(128)S(1)}, f32[64]{0:T(128)}, u32[]{:S(2)}) copy-start(f32[64]{0:T(128)} %param.22) | copy-start | bytes 772
  13.6 166.5 %copy-start.39 = (s32[1,4]{1,0:T(1,128)S(1)}, s32[1,4]{1,0:T(1,128)}, u32[]{:S(2)}) copy-start(s32[1,4]{1,0:T(1,128)} %param.25) | copy-start | bytes 52
  13.6 231.0 %copy-start.3 = (bf16[1,128,1024]{2,1,0:T(8,128)(2,1)S(1)}, bf16[1,128,1024]{2,1,0:T(8,128)(2,1)}, u32[]{:S(2)}) copy-start(bf16[1,128,1024]{2,1,0:T(8,128)(2,1)} %param.14) | copy-start | bytes 786436
  13.6 230.9 %all-gather.14.cloned.1.call-start = ((), (), s32[]{:S(2)}) async-start(), calls=%async_computation.8 | async-start | bytes 11796480 | tf_op jit(solution)/shard_map/all_gather | solution.py:223
  14.4 398.8 %all-gather.12.cloned.1.call-start = ((), (), s32[]{:S(2)}) async-start(), calls=%async_computation.7 | async-start | bytes 8650752 | tf_op jit(solution)/shard_map/all_gather | solution.py:23
  14.7 163.5 %copy-start.34 = (f32[128]{0:T(128)}, f32[128]{0:T(128)S(1)}, u32[]{:S(2)}) copy-start(f32[128]{0:T(128)S(1)} %fusion.83) | copy-start | bytes 1540
  15.3 238.0 %copy-start.18 = (f32[128,32]{0,1:T(8,128)}, f32[128,32]{0,1:T(8,128)S(1)}, u32[]{:S(2)}) copy-start(f32[128,32]{0,1:T(8,128)S(1)} %get-tuple-element.74) | copy-start | bytes 49156
  178.6 74.6 %copy-start.32 = (f32[64]{0:T(128)S(1)}, f32[64]{0:T(128)}, u32[]{:S(2)}) copy-start(f32[64]{0:T(128)} %param.21) | copy-start | bytes 772
  180.0 583.7 %reduce-scatter.16.cloned.1.call-start = ((), (), s32[]{:S(2)}) async-start(), calls=%async_computation.14 | async-start | bytes 8650752
  253.2 165.8 %copy-start.26 = (f32[128,16]{0,1:T(8,128)}, f32[128,16]{0,1:T(8,128)S(1)}, u32[]{:S(2)}) copy-start(f32[128,16]{0,1:T(8,128)S(1)} %multiply_reduce_fusion.6) | copy-start | bytes 24580
  253.2 165.8 %copy-start.20 = (f32[128,16]{0,1:T(8,128)}, f32[128,16]{0,1:T(8,128)S(1)}, u32[]{:S(2)}) copy-start(f32[128,16]{0,1:T(8,128)S(1)} %fusion.80) | copy-start | bytes 24580
  253.4 171.9 %copy-start.9 = (bf16[128,16,32]{0,2,1:T(8,128)(2,1)}, bf16[128,16,32]{0,2,1:T(8,128)(2,1)S(1)}, u32[]{:S(2)}) copy-start(bf16[128,16,32]{0,2,1:T(8,128)(2,1)S(1)} %get-tuple-element.65) | copy-start | bytes 393220
  253.4 171.9 %copy-start.10 = (bf16[128,16,32]{0,2,1:T(8,128)(2,1)}, bf16[128,16,32]{0,2,1:T(8,128)(2,1)S(1)}, u32[]{:S(2)}) copy-start(bf16[128,16,32]{0,2,1:T(8,128)(2,1)S(1)} %get-tuple-element.66) | copy-start | bytes 393220
  462.0 19.5 %copy-start.30 = (f32[1024]{0:T(1024)S(1)}, f32[1024]{0:T(1024)}, u32[]{:S(2)}) copy-start(f32[1024]{0:T(1024)} %param.23) | copy-start | bytes 12292
  492.5 14.1 copy-start.11
  492.5 14.1 copy-start.13
  571.3 12.1 copy-start.5
  583.3 287.7 %reduce-scatter.12.cloned.1.call-start = ((), (), s32[]{:S(2)}) async-start(), calls=%async_computation.11 | async-start | bytes 11796480 | tf_op jit(solution)/shard_map/reduce_scatter | solution.py:296
  588.6 336.0 %reduce-scatter.8.cloned.1.call-start = ((), (), s32[]{:S(2)}) async-start(), calls=%async_computation.9 | async-start | bytes 5242880 | tf_op jit(solution)/shard_map/reduce_scatter | solution.py:369
  589.0 10.1 copy-start.19
  589.0 10.2 copy-start.21
  589.0 10.2 copy-start.33
  589.0 10.9 copy-start.27
  764.8 13.3 copy-start.16
  773.4 299.8 %reduce-scatter.10.cloned.1.call-start = ((), (), s32[]{:S(2)}) async-start(), calls=%async_computation.10 | async-start | bytes 23592960 | tf_op jit(solution)/shard_map/reduce_scatter | solution.py:305
  792.0 505.9 %reduce-scatter.14.cloned.1.call-start = ((), (), s32[]{:S(2)}) async-start(), calls=%async_computation.12 | async-start | bytes 8921088 | tf_op jit(solution)/shard_map/reduce_scatter | solution.py:44
  1118.5 183.4 %copy-start.37 = (f32[1024]{0:T(1024)S(1)}, f32[1024]{0:T(1024)}, u32[]{:S(2)}) copy-start(f32[1024]{0:T(1024)} %get-tuple-element.44) | copy-start | bytes 12292
  1118.6 544.1 %all-reduce.11.cloned.1.call-start = ((), (), s32[]{:S(2)}) async-start(), calls=%async_computation.15 | async-start | bytes 131072
  1120.3 545.1 %all-gather.16.cloned.1.call-start = ((), (), s32[]{:S(2)}) async-start(), calls=%async_computation.13 | async-start | bytes 8921088 | tf_op jit(solution)/shard_map/all_gather | solution.py:60
  1485.0 176.8 %copy-start.41 = (f32[128]{0:T(128)S(1)}, f32[128]{0:T(128)}, u32[]{:S(2)}) copy-start(f32[128]{0:T(128)} %copy-done.40) | copy-start | bytes 1540
  (21 other events, 82.8 us)
Sparse Core Ops, SparseCore 0:
  13.7 161.4 all-gather.9
  176.9 67.6 all-gather.13
  246.8 166.3 all-gather.11
  583.4 180.2 reduce-scatter.15
  766.3 104.6 reduce-scatter.11
  874.0 50.4 reduce-scatter.7
  927.5 145.7 reduce-scatter.9
  1118.7 179.1 reduce-scatter.13
  1303.5 132.5 all-reduce.10
  1438.3 168.2 all-gather.15
where the time goes:
time: 1800 us; the launch traced here: 1790 us
  waiting for transfers between devices  904 us (50%)
  blocking collectives  401 us (22%)
  local copies, waits for them, and re-layouts  226 us (13%)
  matrix products  160 us (9%)
  other arithmetic  83.4 us (5%)
    all_gather x2, blocking collectives, over_pieces(): pieces = lax.all_gather(array, axis)  347 us
    all_gather x2, waiting for transfers between devices, side_by_side(): lax.all_gather(both, axis, axis=dim, tiled=True)  320 us
    reduce_scatter x1, waiting for transfers between devices, sum_packed(): lax.psum_scatter(lines, axis, tiled=True).reshape(-1)  178 us
    unnamed x12, waiting for transfers between devices  164 us
    reduce_scatter x1, waiting for transfers between devices, per_device(): lax.psum_scatter(jnp.concatenate([outer_sum(ffn_low, gate_low), outer_sum...  140 us
    convert_element_type x8, local copies, waits for them, and re-layouts, per_device(): part.astype(jnp.float32)  67.7 us
    all_gather x1, waiting for transfers between devices, per_device(): lax.all_gather(down_weight, 'fsdp', axis=0, tiled=True)  62.6 us
    all_to_all x1, blocking collectives, summed_on_arrival(): lax.all_to_all(pieces, axis, split_axis=0, concat_axis=0, tiled=True)  54.7 us
  transfers between devices with their start and end apart: 10, of which 8 were waited for; matrix products, arithmetic and copies ran while one was open for 7% of the time, Pallas kernels for 0%

commit v1 on v0

v1 whole, which is shorter than its diff:
```python
import functools
import math

import jax
import jax.numpy as jnp
from jax import lax
from jax.experimental import pallas as pl
from jax.experimental.pallas import tpu as pltpu
from jax.sharding import PartitionSpec as P

QUERY_HEADS = 16
KEY_VALUE_HEADS = 8
HEAD_SIZE = 64
FF = 4608
D = 1024
TOKENS = 128
RING = 32
QUARTER = 8
SLICE = 1152
HALF_FF = FF // 2
KEY_TILE = 512
SEQ = 4096

EPSILON = 1e-05
ROPE_BASE = 1000000.0
SCORE_TO_EXP2 = float(HEAD_SIZE) ** (-0.5) * math.log2(math.e)

MESH = pl.DeviceIdType.MESH
ANY = pl.BlockSpec(memory_space=pl.ANY)
VMEM = pl.BlockSpec(memory_space=pltpu.VMEM)
SMEM = pl.BlockSpec(memory_space=pltpu.SMEM)
BF16 = jnp.bfloat16
F32 = jnp.float32
MIB = 1 << 20


class Place:
    def __init__(self):
        self.ctx, self.fsdp = (lax.axis_index("ctx"), lax.axis_index("fsdp"))
        self.zl, self.x, self.y = (self.ctx // 16, (self.ctx // 4) % 4, self.ctx % 4)
        self.zh, self.core = (self.fsdp // 2, self.fsdp % 2)
        self.z = self.zh * 2 + self.zl

    def device(self, x=None, y=None, z=None, core=None):
        x = self.x if x is None else x
        y = self.y if y is None else y
        z = self.z if z is None else z
        core = self.core if core is None else core
        return ((z % 2) * 16 + x * 4 + y, (z // 2) * 2 + core)

    def sibling(self):
        return self.device(core=1 - self.core)

    def along(self, axis, step):
        coordinate = (getattr(self, axis) + step) % 4
        return coordinate, self.device(**{axis: coordinate})


class Wires:
    def __init__(self, sends, receives, locals_=None):
        self.sends, self.receives, self.locals_ = (sends, receives, locals_)
        self.pushed, self.moved = ([], 0)

    def push(self, source, target, device):
        at = len(self.pushed)
        copy = pltpu.make_async_remote_copy(
            src_ref=source,
            dst_ref=target,
            send_sem=self.sends.at[at],
            recv_sem=self.receives.at[at],
            device_id=device,
            device_id_type=MESH,
        )
        copy.start()
        self.pushed.append(copy)
        return copy

    def move(self, source, target):
        copy = pltpu.make_async_copy(source, target, self.locals_.at[self.moved])
        copy.start()
        self.moved += 1
        return copy

    def finish_sends(self):
        for copy in self.pushed:
            copy.wait_send()


def arrive(copies):
    for copy in copies:
        copy.wait_recv()


def greet(devices):
    barrier = pltpu.get_barrier_semaphore()
    for device in devices:
        pl.semaphore_signal(barrier, inc=1, device_id=device, device_id_type=MESH)
    pl.semaphore_wait(barrier, len(devices))


def wired_call(kernel, outs, ins, collective_id, name, copies, moves, scratch=(), in_specs=None,
               out_specs=None, vmem=32 * MIB):
    return pl.pallas_call(
        kernel,
        out_shape=outs,
        in_specs=[ANY] * len(ins) if in_specs is None else in_specs,
        out_specs=[ANY] * len(outs) if out_specs is None else out_specs,
        scratch_shapes=[
            *scratch,
            pltpu.SemaphoreType.DMA((copies,)),
            pltpu.SemaphoreType.DMA((copies,)),
            pltpu.SemaphoreType.DMA((max(moves, 1),)),
        ],
        compiler_params=pltpu.CompilerParams(
            collective_id=collective_id, has_side_effects=True, vmem_limit_bytes=vmem
        ),
        name=name,
    )(*ins)


def shape(*dims, dtype=BF16):
    return jax.ShapeDtypeStruct(dims, dtype)


def gather_weights_kernel(
    qkv, out, gate, up, down, qkv_all, out_all, gate_all, up_all, down_all, sends, receives, moves
):
    here = Place()
    wires = Wires(sends, receives, moves)
    zh, core, x, y = (here.zh, here.core, here.x, here.y)
    other = 1 - zh
    steps = (1, 3, 2)
    xs = [here.along("x", s)[1] for s in steps]
    ys = [here.along("y", s)[1] for s in steps]
    across = 3 - here.z
    cross = [here.device(z=across, core=(core + t) % 2) for t in range(2)]
    sibling = here.sibling()
    greet(xs + ys + cross + [sibling])

    def ff_columns(r, c):
        return pl.ds(pl.multiple_of(r * HALF_FF + c * SLICE, 128), SLICE)

    def down_columns():
        return pl.ds(pl.multiple_of(y * 256, 256), 256)

    crossed = {}
    crossed["qkv"] = [wires.push(qkv.at[x, y], qkv_all.at[zh, core, x, y], cross[0])]
    crossed["out"] = [wires.push(out.at[x, y], out_all.at[zh, core, x, y], cross[0])]
    for name, shard, whole in (("gate", gate, gate_all), ("up", up, up_all)):
        crossed[name] = [
            wires.push(
                shard.at[x, y, :, ff_columns(r, (core + t) % 2)],
                whole.at[zh, core, x, y, :, pl.ds(r * SLICE, SLICE)],
                cross[t],
            )
            for t in range(2)
            for r in range(2)
        ]
    crossed["down"] = [
        wires.push(
            down.at[x, :, :, down_columns()], down_all.at[zh, x, :, :, down_columns()], cross[0]
        )
    ]
    beside = [
        wires.push(qkv, qkv_all.at[zh, core], sibling),
        wires.push(out, out_all.at[zh, core], sibling),
    ]
    kept = [wires.move(qkv, qkv_all.at[zh, core]), wires.move(out, out_all.at[zh, core])]
    for shard, whole in ((gate, gate_all), (up, up_all)):
        for r in range(2):
            target = whole.at[zh, core, :, :, :, pl.ds(r * SLICE, SLICE)]
            beside.append(wires.push(shard.at[:, :, :, ff_columns(r, 1 - core)], target, sibling))
            kept.append(wires.move(shard.at[:, :, :, ff_columns(r, core)], target))
    kept.append(wires.move(down, down_all.at[zh]))

    def own_piece(name, half):
        if name == "down":
            return down_all.at[other, x, half, :, down_columns()]
        if name in ("gate", "up"):
            whole = gate_all if name == "gate" else up_all
            return whole.at[other, :, x, y, :, pl.ds(half * SLICE, SLICE)]
        whole, width = (qkv_all, 1024) if name == "qkv" else (out_all, 512)
        return whole.at[other, core, x, y, :, pl.ds(half * width, width)]

    def line(name, half):
        if name == "down":
            if half == 0:
                return down_all.at[other, :, 0, :, down_columns()]
            return down_all.at[other, x, 1]
        if name in ("gate", "up"):
            whole = gate_all if name == "gate" else up_all
            if half == 0:
                return whole.at[other, :, :, y, :, pl.ds(0, SLICE)]
            return whole.at[other, :, x, :, :, pl.ds(SLICE, SLICE)]
        whole, width = (qkv_all, 1024) if name == "qkv" else (out_all, 512)
        if half == 0:
            return whole.at[other, core, :, y, :, pl.ds(0, width)]
        return whole.at[other, core, x, :, :, pl.ds(width, width)]

    names = ("qkv", "out", "gate", "up", "down")
    first, second = ({}, {})
    for name in names:
        arrive(crossed[name])
        first[name] = [
            wires.push(own_piece(name, half), own_piece(name, half), device)
            for half, ring in ((0, xs), (1, ys))
            for device in ring
        ]
    for name in names:
        arrive(first[name])
        second[name] = [
            wires.push(line(name, half), line(name, half), device)
            for half, ring in ((0, ys), (1, xs))
            for device in ring
        ]
    for name, whole in (("qkv", qkv_all), ("out", out_all)):
        arrive(second[name])
        beside.append(wires.push(whole.at[other, core], whole.at[other, core], sibling))
    for name in names[2:]:
        arrive(second[name])
    arrive(beside)
    for copy in kept:
        copy.wait()
    wires.finish_sends()


def gather_weights(qkv, out, gate, up, down):
    rows = (4, 4, 16)
    ins = (
        qkv.reshape(*rows, 2048),
        out.reshape(*rows, D),
        gate.reshape(*rows, FF),
        up.reshape(*rows, FF),
        down.reshape(4, 2, 144, D),
    )
    outs = [
        shape(2, 2, *rows, 2048),
        shape(2, 2, *rows, D),
        shape(2, 2, *rows, HALF_FF),
        shape(2, 2, *rows, HALF_FF),
        shape(2, 4, 2, 144, D),
    ]
    copies = 3 + 8 + 6 + 30 + 30 + 2
    qkv, out, gate, up, down = wired_call(
        gather_weights_kernel, outs, ins, 1, "gather_weights", copies, 7
    )
    return (
        qkv.reshape(D, 2048),
        out.reshape(D, D),
        gate.reshape(D, HALF_FF),
        up.reshape(D, HALF_FF),
        down.reshape(HALF_FF, D),
    )


class RowsByShard:
    lead = (2, 2, 4, 4)

    def __init__(self, columns):
        self.columns = columns

    def order(self, at):
        return [at.get("zh"), at.get("zl"), at.get("x"), at.get("y")]

    def tail(self, at):
        return (slice(None), slice(None))

    def tail_dims(self, at):
        return (16, self.columns)


class RowsByPlane:
    lead = (2, 4, 4)

    def __init__(self, first, columns):
        self.first, self.columns = (first, columns)

    def order(self, at):
        return [at.get("zh"), at.get("x"), at.get("y")]

    def tail(self, at):
        if "zl" not in at:
            return (slice(None), pl.ds(self.first, self.columns))
        half = self.columns // 2
        return (slice(None), pl.ds(pl.multiple_of(self.first + half * at["zl"], 128), half))

    def tail_dims(self, at):
        return (16, self.columns // 2 if "zl" in at else self.columns)


class ColumnsByY:
    lead = (2, 4, 2)

    def __init__(self, rows):
        self.rows = rows

    def order(self, at):
        return [at.get("zh"), at.get("x"), at.get("zl")]

    def tail(self, at):
        if "y" not in at:
            return (slice(None), slice(None))
        return (slice(None), pl.ds(pl.multiple_of(at["y"] * 256, 256), 256))

    def tail_dims(self, at):
        return (self.rows, 256 if "y" in at else D)


def view(kind, ref, at, skip=0):
    lead = [slice(None) if i is None else i for i in kind.order(at)[skip:]]
    return ref.at[(*lead, *kind.tail(at))]


def open_dims(kind, at):
    return tuple(n for n, i in zip(kind.lead, kind.order(at)) if i is None)


def fix(at, axis, coordinate):
    if axis == "z":
        return {**at, "zh": coordinate // 2, "zl": coordinate % 2}
    return {**at, axis: coordinate}


PARTS = (
    (0, RowsByShard(HALF_FF), ("z", "x", "y")),
    (1, RowsByShard(HALF_FF), ("x", "y", "z")),
    (2, ColumnsByY(144), ("y", "z", "x")),
    (3, RowsByPlane(0, 1024), ("z", "x", "y")),
    (3, RowsByPlane(1024, 1024), ("x", "y", "z")),
    (4, ColumnsByY(32), ("y", "z", "x")),
)
STEPS = (1, 3, 2)


def slot_shapes():
    found = []
    for _, kind, order in PARTS:
        at = {}
        for axis in order:
            at = fix(at, axis, 0)
            found.append((3, *open_dims(kind, at), *kind.tail_dims(at)))
    return found


def add_up(kind, total, slots, at):
    dims = open_dims(kind, at)
    order = kind.order(at)
    tail = kind.tail(at)

    def body(i, _):
        inner, rest = ([], i)
        for n in reversed(dims):
            inner.insert(0, rest % n)
            rest = rest // n
        picks = iter(inner)
        where = (*[next(picks) if o is None else o for o in order], *tail)
        value = total[where].astype(F32)
        for j in range(3):
            value += slots[(j, *inner, slice(None), slice(None))].astype(F32)
        total[where] = value.astype(BF16)
        return 0

    lax.fori_loop(0, math.prod(dims), body, 0)


def reduce_weights_kernel(*refs):
    grads, gains = (refs[:5], refs[5])
    gate_near, up_near, gate_out, up_out, down_out, qkv_out, out_out, gains_out = refs[6:14]
    totals = refs[14:19]
    slots = refs[19:37]
    gain_slots, sends, receives, moves = refs[37:]
    nears = (gate_near, up_near, down_out, qkv_out, out_out)

    here = Place()
    wires = Wires(sends, receives, moves)
    core = here.core
    sibling = here.sibling()
    ring = {a: [here.along(a, s) for s in STEPS] for a in ("x", "y", "z")}
    greet([device for a in ("x", "y", "z") for _, device in ring[a]] + [sibling])

    gain_slots[0, core] = gains[...]
    gain_copies = [wires.push(gain_slots.at[0, core], gain_slots.at[0, core], sibling)]

    def next_gains(stage):
        arrive(gain_copies)
        total = gain_slots[stage, 0] + gain_slots[stage, 1]
        if stage > 0:
            total = total + gain_slots[stage, 2] + gain_slots[stage, 3]
        if stage == 3:
            gains_out[...] = total
            return
        axis = ("x", "y", "z")[stage]
        me = getattr(here, axis)
        gain_slots[stage + 1, me] = total
        source = gain_slots.at[stage + 1, me]
        gain_copies[:] = [wires.push(source, source, device) for _, device in ring[axis]]

    fixed = [{} for _ in PARTS]
    flying = [None] * len(PARTS)
    own = [None] * len(PARTS)
    for step in range(3):
        for p, (g, kind, order) in enumerate(PARTS):
            if step > 0:
                if own[p] is not None:
                    own[p].wait()
                    own[p] = None
                arrive(flying[p])
                add_up(kind, totals[g], slots[3 * p + step - 1], fixed[p])
            axis = order[step]
            source = grads[g] if step == 0 else totals[g]
            flying[p] = [
                wires.push(
                    view(kind, source, fix(fixed[p], axis, coordinate)),
                    slots[3 * p + step].at[j],
                    device,
                )
                for j, (coordinate, device) in enumerate(ring[axis])
            ]
            fixed[p] = fix(fixed[p], axis, getattr(here, axis))
            if step == 0:
                own[p] = wires.move(
                    view(kind, source, fixed[p]), view(kind, totals[g], fixed[p])
                )
        next_gains(step)
    next_gains(3)

    for p, (g, kind, order) in enumerate(PARTS):
        arrive(flying[p])
        add_up(kind, totals[g], slots[3 * p + 2], fixed[p])
        own[p] = wires.move(view(kind, totals[g], fixed[p]), view(kind, nears[g], fixed[p], 1))
    for step in (2, 1, 0):
        for p, (g, kind, order) in enumerate(PARTS):
            if step == 2:
                own[p].wait()
            else:
                arrive(flying[p])
            axis = order[step]
            piece = view(kind, nears[g], fixed[p], 1)
            if axis == "z":
                devices = [here.device(z=here.zh * 2 + 1 - here.zl)]
                gone = ("zl",)
            else:
                devices = [device for _, device in ring[axis]]
                gone = (axis,)
            flying[p] = [wires.push(piece, piece, device) for device in devices]
            fixed[p] = {a: i for a, i in fixed[p].items() if a not in gone}
    last = []
    kept = []
    for p, (near, final) in enumerate(((gate_near, gate_out), (up_near, up_out))):
        arrive(flying[p])
        for r in range(2):
            source = pl.ds(r * SLICE, SLICE)
            target = final.at[:, :, :, pl.ds(pl.multiple_of(r * HALF_FF + core * SLICE, 128), SLICE)]
            last.append(wires.push(near.at[1 - core, :, :, :, source], target, sibling))
            kept.append(wires.move(near.at[core, :, :, :, source], target))
    for p in range(2, len(PARTS)):
        arrive(flying[p])
    arrive(last)
    for copy in kept:
        copy.wait()
    wires.finish_sends()


def reduce_weights(gate, up, down, qkv, out, gains):
    dims = (
        (2, 2, 4, 4, 16, HALF_FF),
        (2, 2, 4, 4, 16, HALF_FF),
        (2, 4, 2, 144, D),
        (2, 4, 4, 16, 2048),
        (2, 4, 2, 32, D),
    )
    ins = [a.reshape(d) for a, d in zip((gate, up, down, qkv, out), dims)] + [gains]
    outs = [
        shape(*dims[0][1:]),
        shape(*dims[1][1:]),
        shape(4, 4, 16, FF),
        shape(4, 4, 16, FF),
        shape(*dims[2][1:]),
        shape(*dims[3][1:]),
        shape(*dims[4][1:]),
        shape(*gains.shape, dtype=F32),
    ]
    scratch = [pltpu.VMEM(d, BF16) for d in dims]
    scratch += [pltpu.VMEM(s, BF16) for s in slot_shapes()]
    scratch += [pltpu.VMEM((4, 4, *gains.shape), F32)]
    copies = 1 + 9 + 6 * 9 + 6 * 7 + 4
    done = wired_call(
        reduce_weights_kernel,
        outs,
        ins,
        2,
        "reduce_weights",
        copies,
        12 + 4,
        scratch,
        [ANY] * 5 + [VMEM],
        [ANY] * 7 + [VMEM],
        vmem=56 * MIB,
    )
    gate, up, down, qkv, out, gains = done[2:]
    return (
        qkv.reshape(256, 2048),
        out.reshape(256, D),
        gate.reshape(256, FF),
        up.reshape(256, FF),
        down.reshape(SLICE, D),
        gains,
    )


def head_columns(head):
    return pl.ds(pl.multiple_of(head * 128, 128), 128)


def to_heads_kernel(with_keys, *refs):
    if with_keys:
        query, key_value, query_out, key_value_out, sends, receives, moves = refs
    else:
        query, query_out, sends, receives, moves = refs
    here = Place()
    wires = Wires(sends, receives, moves)
    me = here.ctx
    quarter, seat = (me // QUARTER, me % QUARTER)
    near = [quarter * QUARTER + (seat + s) % QUARTER for s in range(1, QUARTER)]
    far = [(me + s) % RING for s in range(1, RING)]
    greet([(k, here.fsdp) for k in (far if with_keys else near)])
    copies = [
        wires.push(query.at[:, head_columns(k % QUARTER)], query_out.at[seat], (k, here.fsdp))
        for k in near
    ]
    kept = [wires.move(query.at[:, head_columns(seat)], query_out.at[seat])]
    if with_keys:
        copies += [
            wires.push(
                key_value.at[:, head_columns(k % QUARTER)], key_value_out.at[me], (k, here.fsdp)
            )
            for k in far
        ]
        kept.append(wires.move(key_value.at[:, head_columns(seat)], key_value_out.at[me]))
    arrive(copies)
    for copy in kept:
        copy.wait()
    wires.finish_sends()


def to_heads(query, key_value=None):
    ins = [query] + ([] if key_value is None else [key_value])
    outs = [shape(QUARTER, TOKENS, 128)]
    if key_value is not None:
        outs.append(shape(RING, TOKENS, 128))
    copies = 7 if key_value is None else 38
    return wired_call(
        functools.partial(to_heads_kernel, key_value is not None),
        outs,
        ins,
        3 if key_value is None else 4,
        "to_heads",
        copies,
        2,
    )


def to_tokens_kernel(with_keys, *refs):
    if with_keys:
        query, key_value, query_out, key_value_out, sends, receives, moves = refs
    else:
        query, query_out, sends, receives, moves = refs
    here = Place()
    wires = Wires(sends, receives, moves)
    me = here.ctx
    quarter, seat = (me // QUARTER, me % QUARTER)
    near = [quarter * QUARTER + (seat + s) % QUARTER for s in range(1, QUARTER)]
    far = [(me + s) % RING for s in range(1, RING)]
    greet([(k, here.fsdp) for k in (far if with_keys else near)])
    columns = query_out.at[:, head_columns(seat)]
    copies = [wires.push(query.at[k % QUARTER], columns, (k, here.fsdp)) for k in near]
    kept = [wires.move(query.at[seat], columns)]
    if with_keys:
        copies += [
            wires.push(key_value.at[k], key_value_out.at[me], (k, here.fsdp)) for k in far
        ]
        kept.append(wires.move(key_value.at[me], key_value_out.at[me]))
    arrive(copies)
    for copy in kept:
        copy.wait()
    wires.finish_sends()


def to_tokens(query, key_value=None):
    ins = [query] + ([] if key_value is None else [key_value])
    outs = [shape(TOKENS, D)]
    if key_value is not None:
        outs.append(shape(RING, TOKENS, 128))
    copies = 7 if key_value is None else 38
    return wired_call(
        functools.partial(to_tokens_kernel, key_value is not None),
        outs,
        ins,
        5 if key_value is None else 6,
        "to_tokens",
        copies,
        2,
    )


def half_columns(r, core):
    return pl.ds(pl.multiple_of(r * 512 + core * 256, 256), 256)


def share_kernel(whole, halved, *refs):
    n = whole + halved
    ins, outs = (refs[:n], refs[n : 2 * n])
    here = Place()
    wires = Wires(*refs[2 * n :])
    core = here.core
    sibling = here.sibling()
    greet([sibling])
    copies, kept = ([], [])
    for source, target in zip(ins[:whole], outs[:whole]):
        copies.append(wires.push(source, target.at[core], sibling))
        kept.append(wires.move(source, target.at[core]))
    for source, target in zip(ins[whole:], outs[whole:]):
        for r in range(2):
            place = target.at[core, :, pl.ds(r * 256, 256)]
            copies.append(wires.push(source.at[:, half_columns(r, 1 - core)], place, sibling))
            kept.append(wires.move(source.at[:, half_columns(r, core)], place))
    arrive(copies)
    for copy in kept:
        copy.wait()
    wires.finish_sends()


def share(whole, halved, collective_id):
    outs = [shape(2, *a.shape, dtype=a.dtype) for a in whole]
    outs += [shape(2, a.shape[0], 512, dtype=a.dtype) for a in halved]
    count = len(whole) + 2 * len(halved)
    done = wired_call(
        functools.partial(share_kernel, len(whole), len(halved)),
        outs,
        [*whole, *halved],
        collective_id,
        "share",
        count,
        count,
    )
    return [a.reshape(2 * a.shape[1], a.shape[2]) for a in done]


def hand_over_kernel(count, *refs):
    ins, outs = (refs[:count], refs[count : 2 * count])
    here = Place()
    wires = Wires(*refs[2 * count :])
    sibling = here.sibling()
    greet([sibling])
    copies = [wires.push(i.at[1 - here.core], o, sibling) for i, o in zip(ins, outs)]
    arrive(copies)
    wires.finish_sends()


def hand_over(partials, collective_id):
    return wired_call(
        functools.partial(hand_over_kernel, len(partials)),
        [shape(*a.shape[1:], dtype=a.dtype) for a in partials],
        partials,
        collective_id,
        "hand_over",
        len(partials),
        0,
    )


def nt(left, right):
    return lax.dot_general(left, right, (((1,), (1,)), ((), ())), preferred_element_type=F32)


def nn(left, right):
    return lax.dot_general(left, right, (((1,), (0,)), ((), ())), preferred_element_type=F32)


def by_position(order_ref, key_value_ref, sorted_ref):
    def body(j, _):
        sorted_ref[pl.ds(pl.multiple_of(order_ref[j] * 64, 64), 64), :] = key_value_ref[j]
        return 0

    lax.fori_loop(0, 64, body, 0)


def query_block(ref, t):
    block = ref[t].astype(F32)
    both = jnp.concatenate([block, pltpu.roll(block, 64, 1)], axis=0)
    low = lax.broadcasted_iota(jnp.int32, (128, 128), 1) < 64
    return jnp.where(low, both, 0.0)


def key_limits(order_ref, starts_ref, place_ref, t):
    first = order_ref[place_ref[0] * 16 + t] * 64
    begin = jnp.int32(0)
    for n in range(4):
        begin = jnp.maximum(begin, jnp.where(starts_ref[n] <= first, starts_ref[n], 0))
    return first, begin // KEY_TILE, (first + 63) // KEY_TILE + 1


def first_allowed(position, starts_ref):
    begin = jnp.zeros_like(position)
    for n in range(4):
        begin = jnp.maximum(begin, jnp.where(starts_ref[n] <= position, starts_ref[n], 0))
    return begin


def attend_kernel(
    order_ref, starts_ref, place_ref, query_ref, key_value_ref, out_ref, exact_ref, sum_ref,
    sorted_ref, value_ref,
):
    by_position(order_ref, key_value_ref, sorted_ref)

    def values(j, _):
        rows = pl.ds(pl.multiple_of(j * 256, 256), 256)
        block = pltpu.roll(sorted_ref[rows, :].astype(F32), 64, 1)
        low = lax.broadcasted_iota(jnp.int32, (256, 128), 1) < 64
        value_ref[rows, :] = jnp.where(low, block, 1.0).astype(BF16)
        return 0

    lax.fori_loop(0, SEQ // 256, values, 0)

    def block(t, _):
        first, begin_tile, end_tile = key_limits(order_ref, starts_ref, place_ref, t)
        queries = query_block(query_ref, t).astype(BF16)
        position = first + lax.broadcasted_iota(jnp.int32, (128, 1), 0) % 64
        begin = first_allowed(position, starts_ref)

        def tile(j, total):
            rows = pl.ds(pl.multiple_of(j * KEY_TILE, KEY_TILE), KEY_TILE)
            scores = nt(queries, sorted_ref[rows, :])
            key = j * KEY_TILE + lax.broadcasted_iota(jnp.int32, (128, KEY_TILE), 1)
            allowed = (key <= position) & (key >= begin)
            weight = jnp.where(allowed, jnp.exp2(scores * SCORE_TO_EXP2), 0.0)
            return total + nn(weight.astype(BF16), value_ref[rows, :])

        total = lax.fori_loop(begin_tile, end_tile, tile, jnp.zeros((128, 128), F32))
        sums = pltpu.roll(total, 64, 1)
        attended = total / sums
        low_pair = lax.broadcasted_iota(jnp.int32, (128, 128), 1) < 64
        low = lax.broadcasted_iota(jnp.int32, (64, 128), 1) < 64
        exact_ref[t] = jnp.where(low_pair, attended, 0.0)
        out_ref[t] = jnp.where(low, attended[:64], pltpu.roll(attended[64:], 64, 1)).astype(BF16)
        sum_ref[t] = jnp.transpose(total)[64:72]
        return 0

    lax.fori_loop(0, 16, block, 0)


def attend(order, starts, place, queries, key_values):
    return pl.pallas_call(
        attend_kernel,
        out_shape=[shape(16, 64, 128), shape(16, 128, 128, dtype=F32), shape(16, 8, 128, dtype=F32)],
        in_specs=[SMEM, SMEM, SMEM, VMEM, VMEM],
        out_specs=[VMEM] * 3,
        scratch_shapes=[pltpu.VMEM((SEQ, 128), BF16), pltpu.VMEM((SEQ, 128), BF16)],
        compiler_params=pltpu.CompilerParams(vmem_limit_bytes=32 * MIB),
        name="attend",
    )(order, starts, place, queries, key_values)


def attend_back_kernel(
    order_ref, starts_ref, place_ref, query_ref, key_value_ref, grad_ref, exact_ref, sum_ref,
    query_grad_ref, key_value_grad_ref, sorted_ref, across_ref, total_ref,
):
    by_position(order_ref, key_value_ref, sorted_ref)
    total_ref[...] = jnp.zeros_like(total_ref)

    def turn(j, _):
        rows = pl.ds(pl.multiple_of(j * 128, 128), 128)
        across_ref[:, rows] = jnp.transpose(sorted_ref[rows, :].astype(F32)).astype(BF16)
        return 0

    lax.fori_loop(0, SEQ // 128, turn, 0)

    def block(t, _):
        first, begin_tile, end_tile = key_limits(order_ref, starts_ref, place_ref, t)
        queries = query_block(query_ref, t)
        grads = query_block(grad_ref, t)
        delta = jnp.sum(jnp.transpose(grads * exact_ref[t]), axis=0, keepdims=True)
        total_exp2 = jnp.log2(sum_ref[t][0:1])
        both = jnp.concatenate([queries, pltpu.roll(grads, 64, 1)], axis=0).astype(BF16)
        position = first + lax.broadcasted_iota(jnp.int32, (1, 128), 1) % 64
        begin = first_allowed(position, starts_ref)

        def tile(j, query_grad):
            rows = pl.ds(pl.multiple_of(j * KEY_TILE, KEY_TILE), KEY_TILE)
            products = nt(sorted_ref[rows, :], both)
            key = j * KEY_TILE + lax.broadcasted_iota(jnp.int32, (KEY_TILE, 128), 0)
            allowed = (key <= position) & (key >= begin)
            prob = jnp.where(
                allowed, jnp.exp2(products[:, :128] * SCORE_TO_EXP2 - total_exp2), 0.0
            )
            score = (prob * (products[:, 128:] - delta)).astype(BF16)
            pair = jnp.concatenate([score, prob.astype(BF16)], axis=1)
            total_ref[rows, :] += nn(pair, both)
            return query_grad + nn(across_ref[:, rows], score)

        query_grad = lax.fori_loop(begin_tile, end_tile, tile, jnp.zeros((128, 128), F32))
        query_grad = jnp.transpose(query_grad) * float(HEAD_SIZE) ** (-0.5)
        low = lax.broadcasted_iota(jnp.int32, (64, 128), 1) < 64
        query_grad_ref[t] = jnp.where(
            low, query_grad[:64], pltpu.roll(query_grad[64:], 64, 1)
        ).astype(BF16)
        return 0

    lax.fori_loop(0, 16, block, 0)

    def put_back(j, _):
        rows = pl.ds(pl.multiple_of(order_ref[j] * 64, 64), 64)
        low = lax.broadcasted_iota(jnp.int32, (64, 128), 1) < 64
        scale = jnp.where(low, float(HEAD_SIZE) ** (-0.5), 1.0)
        key_value_grad_ref[j] = (total_ref[rows, :] * scale).astype(BF16)
        return 0

    lax.fori_loop(0, 64, put_back, 0)


def attend_back(order, starts, place, queries, key_values, grads, exact, sums):
    return pl.pallas_call(
        attend_back_kernel,
        out_shape=[shape(16, 64, 128), shape(64, 64, 128)],
        in_specs=[SMEM] * 3 + [VMEM] * 5,
        out_specs=[VMEM] * 2,
        scratch_shapes=[
            pltpu.VMEM((SEQ, 128), BF16),
            pltpu.VMEM((128, SEQ), BF16),
            pltpu.VMEM((SEQ, 128), F32),
        ],
        compiler_params=pltpu.CompilerParams(vmem_limit_bytes=40 * MIB),
        name="attend_back",
    )(order, starts, place, queries, key_values, grads, exact, sums)


def rms_norm(values, gain_row):
    return (
        values * lax.rsqrt(jnp.mean(values * values, axis=-1, keepdims=True) + EPSILON) * gain_row
    )


def rotate(values, positions):
    half_width = values.shape[-1] // 2
    frequency = ROPE_BASE ** (-2.0 * jnp.arange(half_width, dtype=F32) / values.shape[-1])
    angles = positions.astype(F32)[:, None] * frequency[None, :]
    cosine = jnp.cos(angles)[:, None, :]
    sine_part = jnp.sin(angles)[:, None, :]
    first_half = values[..., :half_width]
    second_half = values[..., half_width:]
    return jnp.concatenate(
        [
            first_half * cosine - second_half * sine_part,
            second_half * cosine + first_half * sine_part,
        ],
        axis=-1,
    )


def outer_sum(left, right):
    return lax.dot_general(
        left, right, (((0,), (0,)), ((), ())), preferred_element_type=F32
    ).astype(BF16)


def matmul(left, right):
    return jnp.dot(left, right, preferred_element_type=F32)


def positions_at(block_order, first_row, total_row_count, half_rows):
    row_ids = first_row + jnp.arange(total_row_count, dtype=jnp.int32)
    blocks = row_ids // half_rows
    lookup = jnp.arange(block_order.shape[0], dtype=jnp.int32)
    picked = jnp.sum(jnp.where(blocks[:, None] == lookup[None, :], block_order[None, :], 0), axis=1)
    return picked * half_rows + row_ids % half_rows


def per_device(
    inputs,
    cotangent,
    qkv_weight,
    out_weight,
    gate_weight,
    up_weight,
    down_weight,
    gain_attn,
    gain_query,
    gain_key,
    gain_ffn,
    block_order,
    doc_starts,
):
    cycle_index = lax.axis_index("ctx")
    core = lax.axis_index("fsdp") % 2
    qkv_all, out_all, gate_all, up_all, down_all = gather_weights(
        qkv_weight, out_weight, gate_weight, up_weight, down_weight
    )
    starts = doc_starts[0]
    place = (cycle_index // QUARTER).astype(jnp.int32).reshape(1)
    positions = positions_at(block_order, cycle_index * TOKENS, TOKENS, TOKENS // 2)

    resid_in = inputs[0].astype(F32)
    normed, norm_in_pull = jax.vjp(rms_norm, resid_in, gain_attn)
    normed_low = normed.astype(BF16)
    projected = matmul(normed_low, qkv_all)
    split_position = (QUERY_HEADS + KEY_VALUE_HEADS) * HEAD_SIZE

    def query_key(leading_columns, scale_query, scale_key):
        queries = leading_columns[:, : QUERY_HEADS * HEAD_SIZE].reshape(
            TOKENS, QUERY_HEADS, HEAD_SIZE
        )
        keys = leading_columns[:, QUERY_HEADS * HEAD_SIZE :].reshape(
            TOKENS, KEY_VALUE_HEADS, HEAD_SIZE
        )
        return (
            rotate(rms_norm(queries, scale_query), positions),
            rotate(rms_norm(keys, scale_key), positions),
        )

    (queries, keys), qk_pull = jax.vjp(
        query_key, projected[:, :split_position], gain_query, gain_key
    )
    values = projected[:, split_position:].reshape(TOKENS, KEY_VALUE_HEADS, HEAD_SIZE)
    key_values = jnp.concatenate([keys, values], axis=-1).astype(BF16).reshape(TOKENS, D)
    query_part, key_value_part = to_heads(queries.astype(BF16).reshape(TOKENS, D), key_values)
    query_part = query_part.reshape(16, 64, 128)
    key_value_part = key_value_part.reshape(64, 64, 128)
    attended, exact, sums = attend(block_order, starts, place, query_part, key_value_part)
    (attended_low,) = to_tokens(attended.reshape(QUARTER, TOKENS, 128))

    residual = resid_in + matmul(attended_low, out_all)
    normed_ffn, norm_ffn_pull = jax.vjp(rms_norm, residual, gain_ffn)
    grad_out = cotangent[0]
    ffn_pair, cotangent_pair, normed_half, attended_half = share(
        [normed_ffn.astype(BF16), grad_out], [normed_low, attended_low], 7
    )
    gate_proj = matmul(ffn_pair, gate_all)
    up_proj = matmul(ffn_pair, up_all)
    hidden, gating_pull = jax.vjp(
        lambda gate_in, up_in: jax.nn.silu(gate_in) * up_in, gate_proj, up_proj
    )
    hidden_low = hidden.astype(BF16)
    out_partial = matmul(hidden_low, down_all).reshape(2, TOKENS, D)
    grad_hidden = matmul(cotangent_pair, down_all.T)
    grad_gate, grad_up = gating_pull(grad_hidden)
    gate_low = grad_gate.astype(BF16)
    up_low = grad_up.astype(BF16)
    ffn_partial = (matmul(gate_low, gate_all.T) + matmul(up_low, up_all.T)).reshape(2, TOKENS, D)
    out_rest, ffn_rest = hand_over([out_partial, ffn_partial], 8)

    def mine(pair):
        return lax.dynamic_index_in_dim(pair, core, 0, keepdims=False)

    outputs = residual + mine(out_partial) + out_rest
    grad_resid_ffn, grad_gain_ffn = norm_ffn_pull(mine(ffn_partial) + ffn_rest)
    grad_resid = grad_out.astype(F32) + grad_resid_ffn
    branch_low = grad_resid.astype(BF16)
    grad_attended = matmul(branch_low, out_all.T).astype(BF16)
    (grad_part,) = to_heads(grad_attended)
    query_grad, key_value_grad = attend_back(
        block_order,
        starts,
        place,
        query_part,
        key_value_part,
        grad_part.reshape(16, 64, 128),
        exact,
        sums,
    )
    query_grad, key_value_grad = to_tokens(
        query_grad.reshape(QUARTER, TOKENS, 128), key_value_grad.reshape(RING, TOKENS, 128)
    )
    key_value_grad = key_value_grad.reshape(4, KEY_VALUE_HEADS, TOKENS, 128)
    key_value_grad = jnp.transpose(jnp.sum(key_value_grad.astype(F32), axis=0), (1, 0, 2))
    grad_front, grad_gain_query, grad_gain_key = qk_pull(
        (
            query_grad.astype(F32).reshape(TOKENS, QUERY_HEADS, HEAD_SIZE),
            key_value_grad[..., :HEAD_SIZE],
        )
    )
    grad_values = key_value_grad[..., HEAD_SIZE:].reshape(TOKENS, KEY_VALUE_HEADS * HEAD_SIZE)
    grad_projected = jnp.concatenate([grad_front, grad_values], axis=1).astype(BF16)
    grad_normed = matmul(grad_projected, qkv_all.T)
    grad_input_norm, grad_gain_attn = norm_in_pull(grad_normed)
    grad_inputs = (grad_resid + grad_input_norm).astype(BF16)

    projected_pair, branch_pair = share([grad_projected, branch_low], [], 9)
    gains = jnp.concatenate([grad_gain_attn, grad_gain_ffn, grad_gain_query, grad_gain_key])
    gains = jnp.pad(gains, (0, 24 * 128 - gains.shape[0])).reshape(24, 128)
    grad_qkv, grad_out_weight, grad_gate_weight, grad_up_weight, grad_down, gains = reduce_weights(
        outer_sum(ffn_pair, gate_low),
        outer_sum(ffn_pair, up_low),
        outer_sum(hidden_low, cotangent_pair),
        outer_sum(normed_half, projected_pair),
        outer_sum(attended_half, branch_pair),
        gains,
    )
    gains = gains.reshape(-1)
    return (
        outputs.astype(BF16)[None],
        grad_inputs[None],
        grad_qkv.astype(F32),
        grad_out_weight.astype(F32),
        grad_gate_weight.astype(F32),
        grad_up_weight.astype(F32),
        grad_down.astype(F32),
        gains[:D],
        gains[2 * D : 2 * D + HEAD_SIZE],
        gains[2 * D + HEAD_SIZE : 2 * D + 2 * HEAD_SIZE],
        gains[D : 2 * D],
    )


def solution(mesh):
    in_specs = (
        P("fsdp", "ctx", None),
        P("fsdp", "ctx", None),
        P("fsdp", None),
        P("fsdp", None),
        P("fsdp", None),
        P("fsdp", None),
        P("fsdp", None),
        P(),
        P(),
        P(),
        P(),
        P(),
        P("fsdp", None),
    )
    out_specs = (
        P("fsdp", "ctx", None),
        P("fsdp", "ctx", None),
        P("fsdp", None),
        P("fsdp", None),
        P("fsdp", None),
        P("fsdp", None),
        P("fsdp", None),
        P(),
        P(),
        P(),
        P(),
    )
    return jax.shard_map(
        per_device, mesh=mesh, in_specs=in_specs, out_specs=out_specs, check_vma=False
    )
```

time: 1800 us -> 522 us (0.29)
  waiting for transfers between devices: 904 us -> 0 us
  Pallas kernels: 0 us -> 428 us
  blocking collectives: 401 us -> 0 us
  local copies, waits for them, and re-layouts: 226 us -> 29.1 us
  matrix products: 160 us -> 37.3 us
  other arithmetic: 83.4 us -> 28 us
    pallas_call x0 -> x11, Pallas kernels: none -> 428 us  [the longest x9 370 us: wired_call(): pl.pallas_call(kernel, out_shape=outs, in_specs=[ANY] * len(ins) if in_sp...]
    all_gather x4 -> x0, waiting for transfers between devices: 382 us -> none  [the longest x2 320 us: side_by_side(): lax.all_gather(both, axis, axis=dim, tiled=True)]
    reduce_scatter x4 -> x0, waiting for transfers between devices: 359 us -> none  [the longest x1 178 us: sum_packed(): lax.psum_scatter(lines, axis, tiled=True).reshape(-1)]
    all_gather x2 -> x0, blocking collectives: 347 us -> none  [over_pieces(): pieces = lax.all_gather(array, axis)]
    unnamed x12 -> x0, waiting for transfers between devices: 164 us -> none
    dot_general x16 -> x10, matrix products: 143 us -> 22.9 us  [matmul(): return jnp.dot(left, right, preferred_element_type=F32)]
    convert_element_type x10 -> x2, local copies, waits for them, and re-layouts: 69.6 us -> 1.23 us  [the longest x1 1.08 us: per_device(): jnp.concatenate([keys, values], axis=-1).astype(BF16).reshape(TOKENS, D)]
    all_to_all x1 -> x0, blocking collectives: 54.7 us -> none  [summed_on_arrival(): lax.all_to_all(pieces, axis, split_axis=0, concat_axis=0, tiled=True)]
  transfers between devices with their start and end apart: 10 -> 0, of which waited for: 8 -> 0; matrix products, arithmetic and copies ran while one was open for 7% -> 0% of each run, Pallas kernels for 0% -> 0%
where the time goes in v1:
time: 522 us; the launch traced here: 524 us
  Pallas kernels  428 us (82%)
  matrix products  37.3 us (7%)
  local copies, waits for them, and re-layouts  29.1 us (6%)
  other arithmetic  28 us (5%)
    pallas_call x9, Pallas kernels, wired_call(): pl.pallas_call(kernel, out_shape=outs, in_specs=[ANY] * len(ins) if in_sp...  370 us
    pallas_call x1, Pallas kernels, attend_back(): pl.pallas_call(attend_back_kernel, out_shape=[shape(16, 64, 128), shape(6...  33.3 us
    pallas_call x1, Pallas kernels, attend(): pl.pallas_call(attend_kernel, out_shape=[shape(16, 64, 128), shape(16, 12...  24.6 us
    dot_general x10, matrix products, matmul(): return jnp.dot(left, right, preferred_element_type=F32)  22.9 us
    dot_general x5, matrix products, outer_sum(): lax.dot_general(left, right, (((0,), (0,)), ((), ())), preferred_element_...  14.4 us
    unnamed x146, local copies, waits for them, and re-layouts  11.2 us

profile of v1, /device:TPU:0, one launch (start us, length us, event | category | flops | bytes accessed | tf_op | source)
XLA Modules:
  0.0 524.3 jit_solution(3576942343592828226)
XLA Ops:
  3.0 1.7 copy-done.4
  4.6 1.7 copy-done.5
  6.3 1.7 copy-done.6
  10.2 75.1 %gather_weights.1 = (bf16[2,2,4,4,16,2048]{5,4,3,2,1,0:T(8,128)(2,1)S(1)}, bf16[2,2,4,4,16,1024]{5,4,3,2,1,0:T(8,128)(2,1)S(1)}, bf16[2,2,4,4,16,2304]{5,4,3,2,1...) custom-call(bf16[4,4,16,2048]{3,2,1,0:T(8,128)(2,1)S(1)} %bitcast.172, ...), custom_call_target="tpu_custom_call" | custom-call | tf_op jit(solution)/shard_map/gather_weights/pallas_call | solution.py:103
  85.4 2.2 copy-done.17
  87.6 2.2 fusion.24
  91.6 1.7 slice.67
  100.4 1.7 copy.83
  102.1 1.7 copy.84
  103.8 1.7 pad_maximum_fusion.2
  108.3 20.4 %to_heads.2 = (bf16[8,128,128]{2,1,0:T(8,128)(2,1)S(1)}, bf16[32,128,128]{2,1,0:T(8,128)(2,1)S(1)}) custom-call(bf16[128,1024]{1,0:T(8,128)(2,1)S(1)} %copy.86.refs_0_, bf16[128,1024]{1,0:T(8,128)(2,1)S(1)} %copy.99.refs_1_), custom_call_target="tpu_custom_call" | custom-call | tf_op jit(solution)/shard_map/to_heads/pallas_call | solution.py:103
  128.8 24.6 %attend.1 = (bf16[16,64,128]{2,1,0:T(8,128)(2,1)S(1)}, f32[16,128,128]{2,1,0:T(8,128)S(1)}, f32[16,8,128]{2,1,0:T(8,128)S(1)}) custom-call(s32[64]{0:T(128)S(1)} %copy-done.15, s32[4]{0:T(128)S(1)} %bitcast.183, s32[1]{0:T(128)} %bitcast.2.place_ref, bf16[16,64,128]{2,1,0:T(8,128)(2,1)S(1)} %bitcast.176, bf16[64,64,128]{2,1,0:T(8,128)(2,1)S(1)} %bitcast.164), custom_call_target="tpu_custom_call" | custom-call | tf_op jit(solution)/shard_map/attend/pallas_call | solution.py:753
  153.3 7.3 %to_tokens.2.refs_3_ = bf16[128,1024]{1,0:T(8,128)(2,1)S(1)} custom-call(bf16[8,128,128]{2,1,0:T(8,128)(2,1)S(1)} %bitcast.182), custom_call_target="tpu_custom_call" | custom-call | tf_op jit(solution)/shard_map/to_tokens/pallas_call | solution.py:103
  161.6 2.5 share.2
  164.1 4.0 fusion.38
  168.2 2.8 fusion.37
  171.1 4.2 multiply_convert_fusion
  179.7 2.8 hand_over.1
  185.0 7.8 %to_heads.3 = bf16[8,128,128]{2,1,0:T(8,128)(2,1)S(1)} custom-call(bf16[128,1024]{1,0:T(8,128)(2,1)S(1)} %convolution_convert_fusion.3.refs_0_), custom_call_target="tpu_custom_call" | custom-call | tf_op jit(solution)/shard_map/to_heads/pallas_call | solution.py:103
  192.8 33.3 %attend_back.1 = (bf16[16,64,128]{2,1,0:T(8,128)(2,1)S(1)}, bf16[64,64,128]{2,1,0:T(8,128)(2,1)S(1)}) custom-call(s32[64]{0:T(128)S(1)} %copy-done.15, s32[4]{0:T(128)S(1)} %bitcast.184, s32[1]{0:T(128)} %bitcast.2.place_ref, bf16[16,64,128]{2,1,0:T(8,128)(2,1)S(1)} %bitcast.177, bf16[64,64,128]{2,1,0:T(8,128)(2,1)S(1)} %bitcast.165, ...), custom_call_target="tpu_custom_call" | custom-call | tf_op jit(solution)/shard_map/attend_back/pallas_call | solution.py:822
  226.1 40.3 %to_tokens.3 = (bf16[128,1024]{1,0:T(8,128)(2,1)S(1)}, bf16[32,128,128]{2,1,0:T(8,128)(2,1)S(1)}) custom-call(bf16[8,128,128]{2,1,0:T(8,128)(2,1)S(1)} %bitcast.181, bf16[32,128,128]{2,1,0:T(8,128)(2,1)S(1)} %bitcast.173), custom_call_target="tpu_custom_call" | custom-call | tf_op jit(solution)/shard_map/to_tokens/pallas_call | solution.py:103
  274.5 4.0 fusion.11
  280.5 2.3 share.3
  282.9 2.1 bitcast_convert_fusion
  286.4 3.6 convolution_convert_fusion.1
  290.0 3.6 convolution_convert_fusion.2
  293.7 3.6 convolution_convert_fusion
  297.3 211.7 %reduce_weights.1 = (bf16[2,4,4,16,2304]{4,3,2,1,0:T(8,128)(2,1)}, bf16[2,4,4,16,2304]{4,3,2,1,0:T(8,128)(2,1)}, bf16[4,4,16,4608]{3,2,1,0:T(8,128)(2,1)}, bf16[...) custom-call(bf16[2,2,4,4,16,2304]{5,4,3,2,1,0:T(8,128)(2,1)} %bitcas, ...), custom_call_target="tpu_custom_call" | custom-call | tf_op jit(solution)/shard_map/reduce_weights/pallas_call | solution.py:103
  511.6 2.9 bitcast_convert_fusion.5
  515.6 2.9 bitcast_convert_fusion.3
  518.5 2.9 bitcast_convert_fusion.2
  521.4 2.9 bitcast_convert_fusion.1
  (207 shorter events, 38.7 us)
Async XLA Ops:
  1.8 85.8 %copy-start.58 = (f32[128]{0:T(128)}, f32[128]{0:T(128)S(1)}, u32[]{:S(2)}) copy-start(f32[128]{0:T(128)S(1)} %fusion.32) | copy-start | bytes 1540
  2.7 82.6 %copy-start.40 = (f32[128,32]{0,1:T(8,128)}, f32[128,32]{0,1:T(8,128)S(1)}, u32[]{:S(2)}) copy-start(f32[128,32]{0,1:T(8,128)S(1)} %get-tuple-element.93) | copy-start | bytes 49156
  2.7 82.6 %copy-start.42 = (f32[128,32]{0,1:T(8,128)}, f32[128,32]{0,1:T(8,128)S(1)}, u32[]{:S(2)}) copy-start(f32[128,32]{0,1:T(8,128)S(1)} %get-tuple-element.94) | copy-start | bytes 49156
  10.2 77.4 %copy-start.24 = (bf16[1,128,1024]{2,1,0:T(8,128)(2,1)S(1)}, bf16[1,128,1024]{2,1,0:T(8,128)(2,1)}, u32[]{:S(2)}) copy-start(bf16[1,128,1024]{2,1,0:T(8,128)(2,1)} %param.13) | copy-start | bytes 786436
  10.2 77.4 %copy-start.49 = (f32[1024]{0:T(1024)S(1)}, f32[1024]{0:T(1024)}, u32[]{:S(2)}) copy-start(f32[1024]{0:T(1024)} %param.20) | copy-start | bytes 12292
  94.6 12.0 %copy-start.18 = (f32[128,1024]{0,1:T(8,128)}, f32[128,1024]{0,1:T(8,128)S(1)}, u32[]{:S(2)}) copy-start(f32[128,1024]{0,1:T(8,128)S(1)} %copy.77) | copy-start | bytes 1572868
  98.4 7.1 %copy-start.22 = (f32[128,8,64]{2,0,1:T(8,128)}, f32[128,8,64]{2,0,1:T(8,128)S(1)}, u32[]{:S(2)}) copy-start(f32[128,8,64]{2,0,1:T(8,128)S(1)} %copy.79) | copy-start | bytes 786436
  102.1 26.6 %copy-start.15 = (s32[64]{0:T(128)S(1)}, s32[64]{0:T(128)}, u32[]{:S(2)}) copy-start(s32[64]{0:T(128)} %order_ref.3) | copy-start | bytes 772
  102.1 26.7 %copy-start.16 = (s32[1,4]{1,0:T(1,128)S(1)}, s32[1,4]{1,0:T(1,128)}, u32[]{:S(2)}) copy-start(s32[1,4]{1,0:T(1,128)} %param.25) | copy-start | bytes 52
  128.7 32.5 %copy-start.46 = (f32[1024]{0:T(1024)S(1)}, f32[1024]{0:T(1024)}, u32[]{:S(2)}) copy-start(f32[1024]{0:T(1024)} %param.23) | copy-start | bytes 12292
  128.7 32.5 %copy-start.50 = (f32[1024]{0:T(1024)S(1)}, f32[1024]{0:T(1024)}, u32[]{:S(2)}) copy-start(f32[1024]{0:T(1024)} %param.20) | copy-start | bytes 12292
  128.8 32.5 %copy-start.59 = (f32[128]{0:T(128)S(1)}, f32[128]{0:T(128)}, u32[]{:S(2)}) copy-start(f32[128]{0:T(128)} %copy-done.58) | copy-start | bytes 1540
  161.2 22.1 %copy-start.20 = (f32[128,1024]{1,0:T(8,128)}, f32[128,1024]{1,0:T(8,128)S(1)}, u32[]{:S(2)}) copy-start(f32[128,1024]{1,0:T(8,128)S(1)} %get-tuple-element.96) | copy-start | bytes 1572868
  161.3 22.1 %copy-start.55 = (f32[128]{0:T(128)}, f32[128]{0:T(128)S(1)}, u32[]{:S(2)}) copy-start(f32[128]{0:T(128)S(1)} %fusion.33) | copy-start | bytes 1540
  161.6 6.6 %slice-start = ((s8[4718592]{0:T(1024)(128)(4,1)}), s8[4194304]{0:T(1024)(128)(4,1)S(1)}, s32[]{:S(2)}) async-start(s8[4718592]{0:T(1024)(128)(4,1)} %bitcast.185), calls=%async_computation | async-start | bytes 8388608
  164.1 4.1 copy-start.13
  164.1 7.0 %copy-start.9 = (bf16[2,128,1024]{2,1,0:T(8,128)(2,1)}, bf16[2,128,1024]{2,1,0:T(8,128)(2,1)S(1)}, u32[]{:S(2)}) copy-start(bf16[2,128,1024]{2,1,0:T(8,128)(2,1)S(1)} %get-tuple-element.48) | copy-start | bytes 1572868
  164.1 6.9 %slice-start.2 = ((s8[4718592]{0:T(1024)(128)(4,1)}), s8[4194304]{0:T(1024)(128)(4,1)S(1)}, s32[]{:S(2)}) async-start(s8[4718592]{0:T(1024)(128)(4,1)} %bitcast.207), calls=%async_computation.2 | async-start | bytes 8388608
  168.2 8.6 %slice-start.4 = ((s8[4718592]{0:T(1024)(128)(4,1)}), s8[4194304]{0:T(1024)(128)(4,1)S(1)}, s32[]{:S(2)}) async-start(s8[4718592]{0:T(1024)(128)(4,1)} %bitcast.212), calls=%async_computation.4 | async-start | bytes 8388608
  171.1 5.7 %slice-start.5 = ((s8[4718592]{0:T(1024)(128)(4,1)}), s8[524288]{0:T(1024)(128)(4,1)S(1)}, s32[]{:S(2)}) async-start(s8[4718592]{0:T(1024)(128)(4,1)} %bitcast.212), calls=%async_computation.5 | async-start | bytes 1048576
  183.3 9.5 %copy-start.61 = (f32[128]{0:T(128)}, f32[128]{0:T(128)S(1)}, u32[]{:S(2)}) copy-start(f32[128]{0:T(128)S(1)} %multiply_multiply_fusion.5) | copy-start | bytes 1540
  274.4 4.2 copy-start.66
  274.4 4.2 copy-start.2
  274.5 4.2 copy-start.12
  274.5 4.2 copy-start.21
  274.5 4.2 copy-start.27
  274.5 4.2 copy-start.47
  274.5 4.2 copy-start.51
  274.5 4.2 copy-start.56
  274.5 4.2 copy-start.60
  274.5 4.2 copy-start.62
  508.9 5.6 %copy-start.38 = (bf16[4,2,32,1024]{3,2,1,0:T(8,128)(2,1)S(1)}, bf16[4,2,32,1024]{3,2,1,0:T(8,128)(2,1)}, u32[]{:S(2)}) copy-start(bf16[4,2,32,1024]{3,2,1,0:T(8,128)(2,1)} %get-tuple-element.62) | copy-start | bytes 1572868
  (41 other events, 92.6 us)

commit v2 on v1

--- a/solution.py
+++ b/solution.py
@@ -365,7 +365,7 @@
 
 def reduce_weights_kernel(*refs):
     grads, gains = (refs[:5], refs[5])
-    gate_near, up_near, gate_out, up_out, down_out, qkv_out, out_out, gains_out = refs[6:14]
+    gate_near, up_near, gate_beside, up_beside, down_out, qkv_out, out_out, gains_out = refs[6:14]
     totals = refs[14:19]
     slots = refs[19:37]
     gain_slots, sends, receives, moves = refs[37:]
@@ -445,19 +445,12 @@
             flying[p] = [wires.push(piece, piece, device) for device in devices]
             fixed[p] = {a: i for a, i in fixed[p].items() if a not in gone}
     last = []
-    kept = []
-    for p, (near, final) in enumerate(((gate_near, gate_out), (up_near, up_out))):
+    for p, (near, beside) in enumerate(((gate_near, gate_beside), (up_near, up_beside))):
         arrive(flying[p])
-        for r in range(2):
-            source = pl.ds(r * SLICE, SLICE)
-            target = final.at[:, :, :, pl.ds(pl.multiple_of(r * HALF_FF + core * SLICE, 128), SLICE)]
-            last.append(wires.push(near.at[1 - core, :, :, :, source], target, sibling))
-            kept.append(wires.move(near.at[core, :, :, :, source], target))
+        last.append(wires.push(near.at[1 - core], beside, sibling))
     for p in range(2, len(PARTS)):
         arrive(flying[p])
     arrive(last)
-    for copy in kept:
-        copy.wait()
     wires.finish_sends()
 
 
@@ -473,8 +466,8 @@
     outs = [
         shape(*dims[0][1:]),
         shape(*dims[1][1:]),
-        shape(4, 4, 16, FF),
-        shape(4, 4, 16, FF),
+        shape(*dims[0][2:]),
+        shape(*dims[1][2:]),
         shape(*dims[2][1:]),
         shape(*dims[3][1:]),
         shape(*dims[4][1:]),
@@ -483,7 +476,7 @@
     scratch = [pltpu.VMEM(d, BF16) for d in dims]
     scratch += [pltpu.VMEM(s, BF16) for s in slot_shapes()]
     scratch += [pltpu.VMEM((4, 4, *gains.shape), F32)]
-    copies = 1 + 9 + 6 * 9 + 6 * 7 + 4
+    copies = 1 + 9 + 6 * 9 + 6 * 7 + 2
     done = wired_call(
         reduce_weights_kernel,
         outs,
@@ -491,18 +484,28 @@
         2,
         "reduce_weights",
         copies,
-        12 + 4,
+        12,
         scratch,
         [ANY] * 5 + [VMEM],
         [ANY] * 7 + [VMEM],
         vmem=56 * MIB,
     )
-    gate, up, down, qkv, out, gains = done[2:]
+    core = lax.axis_index("fsdp") % 2
+
+    def joined(near, beside):
+        own = lax.dynamic_index_in_dim(near, core, 0, keepdims=False).reshape(256, HALF_FF)
+        beside = beside.reshape(256, HALF_FF)
+        first, second = (jnp.where(core == 0, own, beside), jnp.where(core == 0, beside, own))
+        pieces = [f[:, r * SLICE : (r + 1) * SLICE] for r in range(2) for f in (first, second)]
+        return jnp.concatenate(pieces, axis=1)
+
+    gate, up = (joined(done[0], done[2]), joined(done[1], done[3]))
+    down, qkv, out, gains = done[4:]
     return (
         qkv.reshape(256, 2048),
         out.reshape(256, D),
-        gate.reshape(256, FF),
-        up.reshape(256, FF),
+        gate,
+        up,
         down.reshape(SLICE, D),
         gains,
     )

time: 522 us -> 447 us (0.86)
  Pallas kernels: 428 us -> 349 us
  local copies, waits for them, and re-layouts: 29.1 us -> 35.2 us
    pallas_call x9, Pallas kernels: 370 us -> 292 us  [wired_call(): pl.pallas_call(kernel, out_shape=outs, in_specs=[ANY] * len(ins) if in_sp...]
    unnamed x146 -> x196, local copies, waits for them, and re-layouts: 11.2 us -> 20.3 us
    dot_general x10, matrix products: 22.9 us -> 17.4 us  [matmul(): return jnp.dot(left, right, preferred_element_type=F32)]
where the time goes in v2:
time: 447 us; the launch traced here: 445 us
  Pallas kernels  349 us (78%)
  local copies, waits for them, and re-layouts  35.2 us (8%)
  matrix products  32.7 us (7%)
  other arithmetic  25.6 us (6%)
    pallas_call x9, Pallas kernels, wired_call(): pl.pallas_call(kernel, out_shape=outs, in_specs=[ANY] * len(ins) if in_sp...  292 us
    pallas_call x1, Pallas kernels, attend_back(): pl.pallas_call(attend_back_kernel, out_shape=[shape(16, 64, 128), shape(6...  32.8 us
    pallas_call x1, Pallas kernels, attend(): pl.pallas_call(attend_kernel, out_shape=[shape(16, 64, 128), shape(16, 12...  24.2 us
    unnamed x196, local copies, waits for them, and re-layouts  20.3 us
    dot_general x10, matrix products, matmul(): return jnp.dot(left, right, preferred_element_type=F32)  17.4 us
    dot_general x5, matrix products, outer_sum(): lax.dot_general(left, right, (((0,), (0,)), ((), ())), preferred_element_...  15.3 us

profile of v2, /device:TPU:0, one launch (start us, length us, event | category | flops | bytes accessed | tf_op | source)
XLA Modules:
  0.0 444.8 jit_solution(11499461615108540346)
XLA Ops:
  0.7 1.7 copy-done.7
  2.3 1.7 copy-done.8
  4.0 1.7 copy-done.9
  7.9 75.1 %gather_weights.1 = (bf16[2,2,4,4,16,2048]{5,4,3,2,1,0:T(8,128)(2,1)S(1)}, bf16[2,2,4,4,16,1024]{5,4,3,2,1,0:T(8,128)(2,1)S(1)}, bf16[2,2,4,4,16,2304]{5,4,3,2,1...) custom-call(bf16[4,4,16,2048]{3,2,1,0:T(8,128)(2,1)S(1)} %bitcast.178, ...), custom_call_target="tpu_custom_call" | custom-call | tf_op jit(solution)/shard_map/gather_weights/pallas_call | solution.py:103
  83.1 2.2 copy-done.28
  91.6 1.8 copy.83
  95.2 1.6 pad_maximum_fusion.2
  102.4 20.1 %to_heads.2 = (bf16[8,128,128]{2,1,0:T(8,128)(2,1)S(1)}, bf16[32,128,128]{2,1,0:T(8,128)(2,1)S(1)}) custom-call(bf16[128,1024]{1,0:T(8,128)(2,1)S(1)} %copy-done.13, bf16[128,1024]{1,0:T(8,128)(2,1)S(1)} %copy.99.refs_1_), custom_call_target="tpu_custom_call" | custom-call | tf_op jit(solution)/shard_map/to_heads/pallas_call | solution.py:103
  124.3 24.2 %attend.1 = (bf16[16,64,128]{2,1,0:T(8,128)(2,1)S(1)}, f32[16,128,128]{2,1,0:T(8,128)S(1)}, f32[16,8,128]{2,1,0:T(8,128)S(1)}) custom-call(s32[64]{0:T(128)S(1)} %copy-done.26, s32[4]{0:T(128)S(1)} %bitcast.189, s32[1]{0:T(128)} %bitcast.2.place_ref, bf16[16,64,128]{2,1,0:T(8,128)(2,1)S(1)} %bitcast.182, bf16[64,64,128]{2,1,0:T(8,128)(2,1)S(1)} %bitcast.170), custom_call_target="tpu_custom_call" | custom-call | tf_op jit(solution)/shard_map/attend/pallas_call | solution.py:756
  149.6 7.2 %to_tokens.2.refs_3_ = bf16[128,1024]{1,0:T(8,128)(2,1)S(1)} custom-call(bf16[8,128,128]{2,1,0:T(8,128)(2,1)S(1)} %bitcast.188), custom_call_target="tpu_custom_call" | custom-call | tf_op jit(solution)/shard_map/to_tokens/pallas_call | solution.py:103
  156.8 1.6 multiply_reduce_fusion.6
  159.3 2.5 share.2
  161.8 1.4 fusion.42
  164.8 2.5 multiply_convert_fusion
  171.6 2.8 hand_over.1
  177.0 2.2 multiply_reduce_fusion.2
  181.2 7.9 %to_heads.3 = bf16[8,128,128]{2,1,0:T(8,128)(2,1)S(1)} custom-call(bf16[128,1024]{1,0:T(8,128)(2,1)S(1)} %convolution_convert_fusion.3.refs_0_), custom_call_target="tpu_custom_call" | custom-call | tf_op jit(solution)/shard_map/to_heads/pallas_call | solution.py:103
  189.2 32.8 %attend_back.1 = (bf16[16,64,128]{2,1,0:T(8,128)(2,1)S(1)}, bf16[64,64,128]{2,1,0:T(8,128)(2,1)S(1)}) custom-call(s32[64]{0:T(128)S(1)} %copy-done.26, s32[4]{0:T(128)S(1)} %bitcast.190, s32[1]{0:T(128)} %bitcast.2.place_ref, bf16[16,64,128]{2,1,0:T(8,128)(2,1)S(1)} %bitcast.183, bf16[64,64,128]{2,1,0:T(8,128)(2,1)S(1)} %bitcast.171, ...), custom_call_target="tpu_custom_call" | custom-call | tf_op jit(solution)/shard_map/attend_back/pallas_call | solution.py:825
  222.0 27.4 %to_tokens.3 = (bf16[128,1024]{1,0:T(8,128)(2,1)S(1)}, bf16[32,128,128]{2,1,0:T(8,128)(2,1)S(1)}) custom-call(bf16[8,128,128]{2,1,0:T(8,128)(2,1)S(1)} %bitcast.187, bf16[32,128,128]{2,1,0:T(8,128)(2,1)S(1)} %bitcast.179), custom_call_target="tpu_custom_call" | custom-call | tf_op jit(solution)/shard_map/to_tokens/pallas_call | solution.py:103
  256.5 4.6 %fusion.11 = (f32[1024]{0:T(1024)S(1)}, f32[128]{0:T(128)S(1)}, f32[128,1024]{1,0:T(8,128)}) fusion(bf16[1,128,1024]{2,1,0:T(8,128)(2,1)S(1)} %copy-done.38, f32[128]{0:T(128)S(1)} %copy-done.86, f32[1024]{0:T(1024)S(1)} %copy-done.74, bf16[1024,2048]{1,0:T(8,128)(2,1)} %bitcast.169, bf16[128,512]{1,0:T(8,128)(2,1)S(1)} %copy.94, ...), kind=kOutput, calls=%fused_computation.39 | convolution fusion | flops 538835840 | bytes 5514240 | tf_op jit(solution)/shard_map/dot_general | solution.py:870
  262.7 2.5 share.3
  265.2 2.4 bitcast_convert_fusion.2
  267.6 2.1 bitcast_convert_fusion
  269.6 3.6 convolution_convert_fusion
  273.3 3.6 convolution_convert_fusion.1
  276.9 3.6 convolution_convert_fusion.2
  280.5 146.7 %reduce_weights.1 = (bf16[2,4,4,16,2304]{4,3,2,1,0:T(8,128)(2,1)}, bf16[2,4,4,16,2304]{4,3,2,1,0:T(8,128)(2,1)}, bf16[4,4,16,2304]{3,2,1,0:T(8,128)(2,1)}, bf16[...) custom-call(bf16[2,2,4,4,16,2304]{5,4,3,2,1,0:T(8,128)(2,1)} %bitcas, ...), custom_call_target="tpu_custom_call" | custom-call | tf_op jit(solution)/shard_map/reduce_weights/pallas_call | solution.py:103
  427.3 1.4 constant_dynamic-slice_fusion.1
  429.4 2.7 maximum_convert_fusion.1
  433.9 2.7 maximum_convert_fusion
  436.7 2.9 bitcast_convert_fusion.1
  439.7 1.6 bitcast_convert_fusion.3
  (265 shorter events, 43.9 us)
Async XLA Ops:
  7.9 77.3 %copy-start.36 = (bf16[1,128,1024]{2,1,0:T(8,128)(2,1)S(1)}, bf16[1,128,1024]{2,1,0:T(8,128)(2,1)}, u32[]{:S(2)}) copy-start(bf16[1,128,1024]{2,1,0:T(8,128)(2,1)} %param.13) | copy-start | bytes 786436
  7.9 78.2 %copy-start.72 = (f32[1024]{0:T(1024)S(1)}, f32[1024]{0:T(1024)}, u32[]{:S(2)}) copy-start(f32[1024]{0:T(1024)} %param.20) | copy-start | bytes 12292
  89.4 8.5 %copy-start.34 = (f32[128,8,64]{2,0,1:T(8,128)}, f32[128,8,64]{2,0,1:T(8,128)S(1)}, u32[]{:S(2)}) copy-start(f32[128,8,64]{2,0,1:T(8,128)S(1)} %copy.79) | copy-start | bytes 786436
  90.7 7.3 %copy-start.57 = (f32[128,32]{1,0:T(8,128)}, f32[128,32]{1,0:T(8,128)S(1)}, u32[]{:S(2)}) copy-start(f32[128,32]{1,0:T(8,128)S(1)} %copy.81) | copy-start | bytes 49156
  91.6 6.3 %slice-start.2 = ((f32[128,2048]{1,0:T(8,128)}), f32[128,1024]{1,0:T(8,128)S(1)}, s32[]{:S(2)}) async-start(f32[128,2048]{1,0:T(8,128)} %copy-done.44), calls=%async_computation.2 | async-start | bytes 1048576 | tf_op jit(solution)/shard_map/jvp()/slice | solution.py:912
  98.0 25.2 %copy-start.27 = (s32[1,4]{1,0:T(1,128)S(1)}, s32[1,4]{1,0:T(1,128)}, u32[]{:S(2)}) copy-start(s32[1,4]{1,0:T(1,128)} %param.25) | copy-start | bytes 52
  123.2 35.2 %copy-start.1 = (bf16[32,128,128]{2,1,0:T(8,128)(2,1)}, bf16[32,128,128]{2,1,0:T(8,128)(2,1)S(1)}, u32[]{:S(2)}) copy-start(bf16[32,128,128]{2,1,0:T(8,128)(2,1)S(1)} %get-tuple-element.43) | copy-start | bytes 3145732
  124.3 34.2 %copy-start.37 = (bf16[1,128,1024]{2,1,0:T(8,128)(2,1)S(1)}, bf16[1,128,1024]{2,1,0:T(8,128)(2,1)}, u32[]{:S(2)}) copy-start(bf16[1,128,1024]{2,1,0:T(8,128)(2,1)} %param.13) | copy-start | bytes 786436
  124.3 34.2 %copy-start.67 = (f32[1024]{0:T(1024)S(1)}, f32[1024]{0:T(1024)}, u32[]{:S(2)}) copy-start(f32[1024]{0:T(1024)} %param.23) | copy-start | bytes 12292
  124.3 34.2 %copy-start.73 = (f32[1024]{0:T(1024)S(1)}, f32[1024]{0:T(1024)}, u32[]{:S(2)}) copy-start(f32[1024]{0:T(1024)} %param.20) | copy-start | bytes 12292
  124.3 34.2 %copy-start.85 = (f32[128]{0:T(128)S(1)}, f32[128]{0:T(128)}, u32[]{:S(2)}) copy-start(f32[128]{0:T(128)} %copy-done.84) | copy-start | bytes 1540
  156.8 5.0 %copy-start.93 = (bf16[2,2,4,4,16,2304]{5,4,3,2,1,0:T(8,128)(2,1)S(1)}, bf16[2,2,4,4,16,2304]{5,4,3,2,1,0:T(8,128)(2,1)}, u32[]{:S(2)}) copy-start(bf16[2,2,4,4,16,2304]{5,4,3,2,1,0:T(8,128)(2,1)} %get-tuple-element.48) | copy-start | bytes 14155780
  158.4 4.8 %copy-start.91 = (f32[128]{0:T(128)}, f32[128]{0:T(128)S(1)}, u32[]{:S(2)}) copy-start(f32[128]{0:T(128)S(1)} %get-tuple-element.111) | copy-start | bytes 1540
  158.4 18.6 %copy-start.78 = (f32[128]{0:T(128)}, f32[128]{0:T(128)S(1)}, u32[]{:S(2)}) copy-start(f32[128]{0:T(128)S(1)} %fusion.33) | copy-start | bytes 1540
  170.2 6.8 %copy-start.68 = (f32[1024]{0:T(1024)S(1)}, f32[1024]{0:T(1024)}, u32[]{:S(2)}) copy-start(f32[1024]{0:T(1024)} %param.23) | copy-start | bytes 12292
  171.6 7.6 %copy-start.92 = (f32[128]{0:T(128)S(1)}, f32[128]{0:T(128)}, u32[]{:S(2)}) copy-start(f32[128]{0:T(128)} %copy-done.91) | copy-start | bytes 1540
  179.2 9.9 %copy-start.42 = (f32[128,1024]{1,0:T(8,128)}, f32[128,1024]{1,0:T(8,128)S(1)}, u32[]{:S(2)}) copy-start(f32[128,1024]{1,0:T(8,128)S(1)} %get-tuple-element.79) | copy-start | bytes 1572868
  179.2 9.9 %copy-start.87 = (f32[128]{0:T(128)}, f32[128]{0:T(128)S(1)}, u32[]{:S(2)}) copy-start(f32[128]{0:T(128)S(1)} %multiply_multiply_fusion.5) | copy-start | bytes 1540
  179.2 9.9 %copy-start.2 = (bf16[32,128,128]{2,1,0:T(8,128)(2,1)S(1)}, bf16[32,128,128]{2,1,0:T(8,128)(2,1)}, u32[]{:S(2)}) copy-start(bf16[32,128,128]{2,1,0:T(8,128)(2,1)} %copy-done.1) | copy-start | bytes 3145732
  179.3 9.9 %copy-start.12 = (f32[16,128,128]{2,1,0:T(8,128)S(1)}, f32[16,128,128]{2,1,0:T(8,128)}, u32[]{:S(2)}) copy-start(f32[16,128,128]{2,1,0:T(8,128)} %copy-done.11) | copy-start | bytes 3145732
  179.3 9.9 %copy-start.16 = (bf16[8,128,128]{2,1,0:T(8,128)(2,1)S(1)}, bf16[8,128,128]{2,1,0:T(8,128)(2,1)}, u32[]{:S(2)}) copy-start(bf16[8,128,128]{2,1,0:T(8,128)(2,1)} %copy-done.14) | copy-start | bytes 786436
  189.2 60.5 %copy-start.58 = (f32[128,32]{1,0:T(8,128)S(1)}, f32[128,32]{1,0:T(8,128)}, u32[]{:S(2)}) copy-start(f32[128,32]{1,0:T(8,128)} %copy-done.57) | copy-start | bytes 49156
  222.0 27.9 %copy-start.35 = (f32[128,8,64]{2,0,1:T(8,128)S(1)}, f32[128,8,64]{2,0,1:T(8,128)}, u32[]{:S(2)}) copy-start(f32[128,8,64]{2,0,1:T(8,128)} %copy-done.34) | copy-start | bytes 786436
  222.0 27.9 %copy-start.71 = (f32[128,8]{0,1:T(8,128)S(1)}, f32[128,8]{0,1:T(8,128)}, u32[]{:S(2)}) copy-start(f32[128,8]{0,1:T(8,128)} %copy-done.70) | copy-start | bytes 12292
  222.0 27.9 %copy-start.82 = (f32[64]{0:T(128)S(1)}, f32[64]{0:T(128)}, u32[]{:S(2)}) copy-start(f32[64]{0:T(128)} %param.22) | copy-start | bytes 772
  256.0 5.0 %copy-start.48 = (bf16[128,1536]{1,0:T(8,128)(2,1)}, bf16[128,1536]{1,0:T(8,128)(2,1)S(1)}, u32[]{:S(2)}) copy-start(bf16[128,1536]{1,0:T(8,128)(2,1)S(1)} %add_convert_fusion) | copy-start | bytes 1179652
  256.4 4.6 %copy-start.77 = (f32[1024]{0:T(1024)S(1)}, f32[1024]{0:T(1024)}, u32[]{:S(2)}) copy-start(f32[1024]{0:T(1024)} %get-tuple-element.73) | copy-start | bytes 12292
  439.6 4.0 copy-start.4
  439.6 4.0 copy-start.19
  439.6 4.0 copy-start.33
  439.6 4.0 copy-start.39
  439.6 4.0 copy-start.43
  (67 other events, 137.2 us)

commit v3 on v2

--- a/solution.py
+++ b/solution.py
@@ -122,105 +122,216 @@
     return jax.ShapeDtypeStruct(dims, dtype)
 
 
+class Pieces:
+    def view(self, ref, at, skip=0):
+        lead = [slice(None) if i is None else i for i in self.order(at)[skip:]]
+        return ref.at[(*lead, *self.tail(at))]
+
+    def open_dims(self, at):
+        return tuple(n for n, i in zip(self.lead, self.order(at)) if i is None)
+
+    def tail(self, at):
+        first, width = self.columns(at)
+        if not isinstance(first, int):
+            first = pl.multiple_of(first, 128)
+        return (slice(None), pl.ds(first, width))
+
+    def tail_dims(self, at):
+        return (self.rows, self.columns(at)[1])
+
+
+def halved(first, width, at):
+    if "half" not in at:
+        return first, width
+    return first + at["half"] * (width // 2), width // 2
+
+
+class RowsByShard(Pieces):
+    lead, rows = ((2, 2, 4, 4), 16)
+
+    def __init__(self, width):
+        self.width = width
+
+    def order(self, at):
+        return [at.get("zh"), at.get("zl"), at.get("x"), at.get("y")]
+
+    def columns(self, at):
+        return halved(0, self.width, at)
+
+
+class RowsByPlane(Pieces):
+    lead, rows = ((2, 4, 4), 16)
+
+    def __init__(self, first, width):
+        self.first, self.width = (first, width)
+
+    def order(self, at):
+        return [at.get("zh"), at.get("x"), at.get("y")]
+
+    def columns(self, at):
+        if "zl" not in at:
+            return halved(self.first, self.width, at)
+        half = self.width // 2
+        return halved(self.first + half * at["zl"], half, at)
+
+
+class ColumnsByY(Pieces):
+    lead = (2, 4, 2)
+
+    def __init__(self, rows):
+        self.rows = rows
+
+    def order(self, at):
+        return [at.get("zh"), at.get("x"), at.get("zl")]
+
+    def columns(self, at):
+        return halved(at["y"] * 256, 256, at) if "y" in at else halved(0, D, at)
+
+
+class ShardsByCore(Pieces):
+    lead, rows = ((2, 2, 4, 4), 16)
+
+    def __init__(self, width):
+        self.width = width
+
+    def order(self, at):
+        return [at.get("zh"), at.get("half"), at.get("x"), at.get("y")]
+
+    def columns(self, at):
+        half = self.width // 2
+        return (half * at["zl"], half) if "zl" in at else (0, self.width)
+
+
+class OneCore(RowsByPlane):
+    lead = (2, 2, 4, 4)
+
+    def __init__(self, width, core):
+        super().__init__(0, width)
+        self.core = core
+
+    def order(self, at):
+        return [at.get("zh"), self.core, at.get("x"), at.get("y")]
+
+
+def fix(at, axis, coordinate):
+    if axis == "z":
+        return {**at, "zh": coordinate // 2, "zl": coordinate % 2}
+    return {**at, axis: coordinate}
+
+
+def without(at, axis):
+    return {a: i for a, i in at.items() if a != ("zl" if axis == "z" else axis)}
+
+
+def in_turn(tasks):
+    while tasks:
+        tasks = [task for task in tasks if next(task, "over") != "over"]
+
+
+def spread(here, wires, kind, ref, at, order, skip=0):
+    for axis in order:
+        piece = kind.view(ref, at, skip)
+        if axis == "z":
+            copies = [wires.push(piece, piece, here.device(z=here.zh * 2 + 1 - here.zl))]
+            yield
+            arrive(copies)
+        else:
+            (_, right), (_, left) = (here.along(axis, 1), here.along(axis, 3))
+            from_left = wires.push(piece, piece, right)
+            from_right = wires.push(piece, piece, left)
+            yield
+            relays = []
+            for half, copy, step, onward in ((0, from_left, 3, right), (1, from_right, 1, left)):
+                arrive([copy])
+                passing = fix(at, axis, here.along(axis, step)[0])
+                passing = kind.view(ref, {**passing, "half": half}, skip)
+                relays.append(wires.push(passing, passing, onward))
+            yield
+            arrive(relays)
+        at = without(at, axis)
+
+
 def gather_weights_kernel(
     qkv, out, gate, up, down, qkv_all, out_all, gate_all, up_all, down_all, sends, receives, moves
 ):
     here = Place()
     wires = Wires(sends, receives, moves)
     zh, core, x, y = (here.zh, here.core, here.x, here.y)
-    other = 1 - zh
-    steps = (1, 3, 2)
-    xs = [here.along("x", s)[1] for s in steps]
-    ys = [here.along("y", s)[1] for s in steps]
+    there = 1 - here.zl
     across = 3 - here.z
     cross = [here.device(z=across, core=(core + t) % 2) for t in range(2)]
     sibling = here.sibling()
-    greet(xs + ys + cross + [sibling])
+    greet([here.along(a, s)[1] for a in ("x", "y") for s in (1, 3)]
+          + [here.device(z=here.zh * 2 + 1 - here.zl), *cross, sibling])
 
     def ff_columns(r, c):
         return pl.ds(pl.multiple_of(r * HALF_FF + c * SLICE, 128), SLICE)
 
-    def down_columns():
-        return pl.ds(pl.multiple_of(y * 256, 256), 256)
-
-    crossed = {}
-    crossed["qkv"] = [wires.push(qkv.at[x, y], qkv_all.at[zh, core, x, y], cross[0])]
-    crossed["out"] = [wires.push(out.at[x, y], out_all.at[zh, core, x, y], cross[0])]
-    for name, shard, whole in (("gate", gate, gate_all), ("up", up, up_all)):
-        crossed[name] = [
+    def part(width):
+        return pl.ds(pl.multiple_of(there * width, 128), width)
+
+    down_columns = pl.ds(pl.multiple_of(y * 256, 256), 256)
+    held = {"zh": 1 - zh, "zl": here.zl, "x": x, "y": y}
+
+    def fetch(kind, whole, crossed, order):
+        yield
+        arrive(crossed)
+        yield from spread(here, wires, kind, whole, held, order)
+
+    def fetch_narrow(shard, whole, width, order):
+        kind = OneCore(width, core)
+        columns = part(width // 2)
+        source = shard.at[x, y, :, columns]
+        crossed = [wires.push(source, whole.at[zh, core, x, y, :, columns], cross[0])]
+        yield from fetch(kind, whole, crossed, order)
+        beside = [wires.push(whole.at[1 - zh, core], whole.at[1 - zh, core], sibling)]
+        yield
+        arrive(beside)
+
+    def fetch_wide(shard, whole, order):
+        crossed = [
             wires.push(
-                shard.at[x, y, :, ff_columns(r, (core + t) % 2)],
-                whole.at[zh, core, x, y, :, pl.ds(r * SLICE, SLICE)],
+                shard.at[x, y, :, ff_columns(there, (core + t) % 2)],
+                whole.at[zh, core, x, y, :, part(SLICE)],
                 cross[t],
             )
             for t in range(2)
-            for r in range(2)
         ]
-    crossed["down"] = [
-        wires.push(
-            down.at[x, :, :, down_columns()], down_all.at[zh, x, :, :, down_columns()], cross[0]
-        )
-    ]
-    beside = [
-        wires.push(qkv, qkv_all.at[zh, core], sibling),
-        wires.push(out, out_all.at[zh, core], sibling),
-    ]
-    kept = [wires.move(qkv, qkv_all.at[zh, core]), wires.move(out, out_all.at[zh, core])]
-    for shard, whole in ((gate, gate_all), (up, up_all)):
-        for r in range(2):
-            target = whole.at[zh, core, :, :, :, pl.ds(r * SLICE, SLICE)]
-            beside.append(wires.push(shard.at[:, :, :, ff_columns(r, 1 - core)], target, sibling))
-            kept.append(wires.move(shard.at[:, :, :, ff_columns(r, core)], target))
-    kept.append(wires.move(down, down_all.at[zh]))
-
-    def own_piece(name, half):
-        if name == "down":
-            return down_all.at[other, x, half, :, down_columns()]
-        if name in ("gate", "up"):
-            whole = gate_all if name == "gate" else up_all
-            return whole.at[other, :, x, y, :, pl.ds(half * SLICE, SLICE)]
-        whole, width = (qkv_all, 1024) if name == "qkv" else (out_all, 512)
-        return whole.at[other, core, x, y, :, pl.ds(half * width, width)]
-
-    def line(name, half):
-        if name == "down":
-            if half == 0:
-                return down_all.at[other, :, 0, :, down_columns()]
-            return down_all.at[other, x, 1]
-        if name in ("gate", "up"):
-            whole = gate_all if name == "gate" else up_all
-            if half == 0:
-                return whole.at[other, :, :, y, :, pl.ds(0, SLICE)]
-            return whole.at[other, :, x, :, :, pl.ds(SLICE, SLICE)]
-        whole, width = (qkv_all, 1024) if name == "qkv" else (out_all, 512)
-        if half == 0:
-            return whole.at[other, core, :, y, :, pl.ds(0, width)]
-        return whole.at[other, core, x, :, :, pl.ds(width, width)]
-
-    names = ("qkv", "out", "gate", "up", "down")
-    first, second = ({}, {})
-    for name in names:
-        arrive(crossed[name])
-        first[name] = [
-            wires.push(own_piece(name, half), own_piece(name, half), device)
-            for half, ring in ((0, xs), (1, ys))
-            for device in ring
+        yield from fetch(ShardsByCore(HALF_FF), whole, crossed, order)
+
+    def fetch_down(order):
+        source = down.at[x, there, :, down_columns]
+        crossed = [wires.push(source, down_all.at[zh, x, there, :, down_columns], cross[0])]
+        yield from fetch(ColumnsByY(144), down_all, crossed, order)
+
+    def from_this_chip():
+        beside, kept = ([], [])
+        for shard, whole in ((qkv, qkv_all), (out, out_all)):
+            beside.append(wires.push(shard, whole.at[zh, core], sibling))
+            kept.append(wires.move(shard, whole.at[zh, core]))
+        for shard, whole in ((gate, gate_all), (up, up_all)):
+            for r in range(2):
+                target = whole.at[zh, core, :, :, :, pl.ds(r * SLICE, SLICE)]
+                source = shard.at[:, :, :, ff_columns(r, 1 - core)]
+                beside.append(wires.push(source, target, sibling))
+                kept.append(wires.move(shard.at[:, :, :, ff_columns(r, core)], target))
+        kept.append(wires.move(down, down_all.at[zh]))
+        for _ in range(6):
+            yield
+        arrive(beside)
+        for copy in kept:
+            copy.wait()
+
+    in_turn(
+        [
+            fetch_narrow(qkv, qkv_all, 2048, ("z", "y", "x")),
+            fetch_wide(gate, gate_all, ("y", "x", "z")),
+            fetch_wide(up, up_all, ("z", "y", "x")),
+            fetch_down(("x", "z", "y")),
+            fetch_narrow(out, out_all, D, ("x", "z", "y")),
+            from_this_chip(),
         ]
-    for name in names:
-        arrive(first[name])
-        second[name] = [
-            wires.push(line(name, half), line(name, half), device)
-            for half, ring in ((0, ys), (1, xs))
-            for device in ring
-        ]
-    for name, whole in (("qkv", qkv_all), ("out", out_all)):
-        arrive(second[name])
-        beside.append(wires.push(whole.at[other, core], whole.at[other, core], sibling))
-    for name in names[2:]:
-        arrive(second[name])
-    arrive(beside)
-    for copy in kept:
-        copy.wait()
+    )
     wires.finish_sends()
 
 
@@ -240,7 +351,7 @@
         shape(2, 2, *rows, HALF_FF),
         shape(2, 4, 2, 144, D),
     ]
-    copies = 3 + 8 + 6 + 30 + 30 + 2
+    copies = 7 + 6 + 5 * 9 + 2
     qkv, out, gate, up, down = wired_call(
         gather_weights_kernel, outs, ins, 1, "gather_weights", copies, 7
     )
@@ -253,114 +364,92 @@
     )
 
 
-class RowsByShard:
-    lead = (2, 2, 4, 4)
-
-    def __init__(self, columns):
-        self.columns = columns
-
-    def order(self, at):
-        return [at.get("zh"), at.get("zl"), at.get("x"), at.get("y")]
-
-    def tail(self, at):
-        return (slice(None), slice(None))
-
-    def tail_dims(self, at):
-        return (16, self.columns)
-
-
-class RowsByPlane:
-    lead = (2, 4, 4)
-
-    def __init__(self, first, columns):
-        self.first, self.columns = (first, columns)
-
-    def order(self, at):
-        return [at.get("zh"), at.get("x"), at.get("y")]
-
-    def tail(self, at):
-        if "zl" not in at:
-            return (slice(None), pl.ds(self.first, self.columns))
-        half = self.columns // 2
-        return (slice(None), pl.ds(pl.multiple_of(self.first + half * at["zl"], 128), half))
-
-    def tail_dims(self, at):
-        return (16, self.columns // 2 if "zl" in at else self.columns)
-
-
-class ColumnsByY:
-    lead = (2, 4, 2)
-
-    def __init__(self, rows):
-        self.rows = rows
-
-    def order(self, at):
-        return [at.get("zh"), at.get("x"), at.get("zl")]
-
-    def tail(self, at):
-        if "y" not in at:
-            return (slice(None), slice(None))
-        return (slice(None), pl.ds(pl.multiple_of(at["y"] * 256, 256), 256))
-
-    def tail_dims(self, at):
-        return (self.rows, 256 if "y" in at else D)
-
-
-def view(kind, ref, at, skip=0):
-    lead = [slice(None) if i is None else i for i in kind.order(at)[skip:]]
-    return ref.at[(*lead, *kind.tail(at))]
-
-
-def open_dims(kind, at):
-    return tuple(n for n, i in zip(kind.lead, kind.order(at)) if i is None)
-
-
-def fix(at, axis, coordinate):
-    if axis == "z":
-        return {**at, "zh": coordinate // 2, "zl": coordinate % 2}
-    return {**at, axis: coordinate}
-
-
 PARTS = (
-    (0, RowsByShard(HALF_FF), ("z", "x", "y")),
-    (1, RowsByShard(HALF_FF), ("x", "y", "z")),
-    (2, ColumnsByY(144), ("y", "z", "x")),
-    (3, RowsByPlane(0, 1024), ("z", "x", "y")),
-    (3, RowsByPlane(1024, 1024), ("x", "y", "z")),
-    (4, ColumnsByY(32), ("y", "z", "x")),
+    (0, RowsByShard(HALF_FF), ("z", "x", "y"), ("y", "x", "z")),
+    (1, RowsByShard(HALF_FF), ("x", "y", "z"), ("z", "y", "x")),
+    (2, ColumnsByY(144), ("y", "z", "x"), ("x", "z", "y")),
+    (3, RowsByPlane(0, 1024), ("z", "x", "y"), ("z", "y", "x")),
+    (3, RowsByPlane(1024, 1024), ("x", "y", "z"), ("x", "z", "y")),
+    (4, ColumnsByY(32), ("y", "z", "x"), ("x", "z", "y")),
 )
-STEPS = (1, 3, 2)
 
 
 def slot_shapes():
     found = []
-    for _, kind, order in PARTS:
+    for _, kind, order, _ in PARTS:
         at = {}
         for axis in order:
             at = fix(at, axis, 0)
-            found.append((3, *open_dims(kind, at), *kind.tail_dims(at)))
+            found.append((6, *kind.open_dims(at), *kind.tail_dims({**at, "half": 0})))
     return found
 
 
-def add_up(kind, total, slots, at):
-    dims = open_dims(kind, at)
-    order = kind.order(at)
-    tail = kind.tail(at)
-
-    def body(i, _):
+def each_block(kind, at, body):
+    dims = kind.open_dims(at)
+
+    def step(i, _):
         inner, rest = ([], i)
         for n in reversed(dims):
             inner.insert(0, rest % n)
             rest = rest // n
         picks = iter(inner)
-        where = (*[next(picks) if o is None else o for o in order], *tail)
-        value = total[where].astype(F32)
-        for j in range(3):
-            value += slots[(j, *inner, slice(None), slice(None))].astype(F32)
-        total[where] = value.astype(BF16)
+        lead = [next(picks) if o is None else o for o in kind.order(at)]
+        body((*lead, *kind.tail(at)), (*inner, slice(None), slice(None)))
         return 0
 
-    lax.fori_loop(0, math.prod(dims), body, 0)
+    lax.fori_loop(0, math.prod(dims), step, 0)
+
+
+def reduce_one(here, wires, kind, grad, total, slots, order):
+    at = {}
+    for step, axis in enumerate(order):
+        source, slot = (grad if step == 0 else total, slots[step])
+        (right_place, right), (left_place, left) = (here.along(axis, 1), here.along(axis, 3))
+        far_place, _ = here.along(axis, 2)
+        mine = fix(at, axis, getattr(here, axis))
+
+        def half_of(place, half):
+            return {**fix(at, axis, place), "half": half}
+
+        relays = [
+            wires.push(kind.view(source, half_of(far_place, 0)), slot.at[4], right),
+            wires.push(kind.view(source, half_of(far_place, 1)), slot.at[5], left),
+        ]
+        arriving = [
+            wires.push(kind.view(source, half_of(right_place, 1)), slot.at[1], right),
+            wires.push(kind.view(source, half_of(left_place, 0)), slot.at[2], left),
+        ]
+        kept = []
+        if step == 0:
+            for where in (half_of(right_place, 0), half_of(left_place, 1), mine):
+                kept.append(wires.move(kind.view(source, where), kind.view(total, where)))
+        yield
+        for j, place, half, target, onward in (
+            (4, right_place, 0, 0, right),
+            (5, left_place, 1, 3, left),
+        ):
+            if kept:
+                kept.pop(0).wait()
+            arrive([relays[j - 4]])
+
+            def pass_on(whole, part):
+                value = slot[(j, *part)].astype(F32) + total[whole].astype(F32)
+                slot[(j, *part)] = value.astype(BF16)
+
+            each_block(kind, half_of(place, half), pass_on)
+            arriving.append(wires.push(slot.at[j], slot.at[target], onward))
+        yield
+        if kept:
+            kept.pop(0).wait()
+        arrive(arriving)
+        for half in range(2):
+
+            def add_up(whole, part):
+                value = total[whole].astype(F32) + slot[(half, *part)].astype(F32)
+                total[whole] = (value + slot[(2 + half, *part)].astype(F32)).astype(BF16)
+
+            each_block(kind, {**mine, "half": half}, add_up)
+        at = mine
 
 
 def reduce_weights_kernel(*refs):
@@ -370,87 +459,49 @@
     slots = refs[19:37]
     gain_slots, sends, receives, moves = refs[37:]
     nears = (gate_near, up_near, down_out, qkv_out, out_out)
+    besides = (gate_beside, up_beside)
 
     here = Place()
     wires = Wires(sends, receives, moves)
     core = here.core
     sibling = here.sibling()
-    ring = {a: [here.along(a, s) for s in STEPS] for a in ("x", "y", "z")}
-    greet([device for a in ("x", "y", "z") for _, device in ring[a]] + [sibling])
-
-    gain_slots[0, core] = gains[...]
-    gain_copies = [wires.push(gain_slots.at[0, core], gain_slots.at[0, core], sibling)]
-
-    def next_gains(stage):
-        arrive(gain_copies)
-        total = gain_slots[stage, 0] + gain_slots[stage, 1]
-        if stage > 0:
-            total = total + gain_slots[stage, 2] + gain_slots[stage, 3]
-        if stage == 3:
-            gains_out[...] = total
-            return
-        axis = ("x", "y", "z")[stage]
-        me = getattr(here, axis)
-        gain_slots[stage + 1, me] = total
-        source = gain_slots.at[stage + 1, me]
-        gain_copies[:] = [wires.push(source, source, device) for _, device in ring[axis]]
-
-    fixed = [{} for _ in PARTS]
-    flying = [None] * len(PARTS)
-    own = [None] * len(PARTS)
-    for step in range(3):
-        for p, (g, kind, order) in enumerate(PARTS):
-            if step > 0:
-                if own[p] is not None:
-                    own[p].wait()
-                    own[p] = None
-                arrive(flying[p])
-                add_up(kind, totals[g], slots[3 * p + step - 1], fixed[p])
-            axis = order[step]
-            source = grads[g] if step == 0 else totals[g]
-            flying[p] = [
-                wires.push(
-                    view(kind, source, fix(fixed[p], axis, coordinate)),
-                    slots[3 * p + step].at[j],
-                    device,
-                )
-                for j, (coordinate, device) in enumerate(ring[axis])
-            ]
-            fixed[p] = fix(fixed[p], axis, getattr(here, axis))
-            if step == 0:
-                own[p] = wires.move(
-                    view(kind, source, fixed[p]), view(kind, totals[g], fixed[p])
-                )
-        next_gains(step)
-    next_gains(3)
-
-    for p, (g, kind, order) in enumerate(PARTS):
-        arrive(flying[p])
-        add_up(kind, totals[g], slots[3 * p + 2], fixed[p])
-        own[p] = wires.move(view(kind, totals[g], fixed[p]), view(kind, nears[g], fixed[p], 1))
-    for step in (2, 1, 0):
-        for p, (g, kind, order) in enumerate(PARTS):
-            if step == 2:
-                own[p].wait()
+    greet([here.along(a, s)[1] for a in ("x", "y", "z") for s in (1, 3, 2)] + [sibling])
+
+    def all_gains():
+        total = gains[...]
+        for stage, axis in enumerate(("core", "x", "y", "z")):
+            me = getattr(here, axis)
+            gain_slots[stage, me] = total
+            source = gain_slots.at[stage, me]
+            if axis == "core":
+                others = [sibling]
             else:
-                arrive(flying[p])
-            axis = order[step]
-            piece = view(kind, nears[g], fixed[p], 1)
-            if axis == "z":
-                devices = [here.device(z=here.zh * 2 + 1 - here.zl)]
-                gone = ("zl",)
-            else:
-                devices = [device for _, device in ring[axis]]
-                gone = (axis,)
-            flying[p] = [wires.push(piece, piece, device) for device in devices]
-            fixed[p] = {a: i for a, i in fixed[p].items() if a not in gone}
-    last = []
-    for p, (near, beside) in enumerate(((gate_near, gate_beside), (up_near, up_beside))):
-        arrive(flying[p])
-        last.append(wires.push(near.at[1 - core], beside, sibling))
-    for p in range(2, len(PARTS)):
-        arrive(flying[p])
-    arrive(last)
+                others = [here.along(axis, s)[1] for s in (1, 3, 2)]
+            copies = [wires.push(source, source, device) for device in others]
+            yield
+            yield
+            arrive(copies)
+            total = gain_slots[stage, 0] + gain_slots[stage, 1]
+            if axis != "core":
+                total = total + gain_slots[stage, 2] + gain_slots[stage, 3]
+        gains_out[...] = total
+
+    def one(p):
+        g, kind, order, back = PARTS[p]
+        yield from reduce_one(
+            here, wires, kind, grads[g], totals[g], slots[3 * p : 3 * p + 3], order
+        )
+        at = {"zh": here.zh, "zl": here.zl, "x": here.x, "y": here.y}
+        own = wires.move(kind.view(totals[g], at), kind.view(nears[g], at, 1))
+        yield
+        own.wait()
+        yield from spread(here, wires, kind, nears[g], at, back, 1)
+        if g < 2:
+            copies = [wires.push(nears[g].at[1 - core], besides[g], sibling)]
+            yield
+            arrive(copies)
+
+    in_turn([all_gains()] + [one(p) for p in range(len(PARTS))])
     wires.finish_sends()
 
 
@@ -476,7 +527,7 @@
     scratch = [pltpu.VMEM(d, BF16) for d in dims]
     scratch += [pltpu.VMEM(s, BF16) for s in slot_shapes()]
     scratch += [pltpu.VMEM((4, 4, *gains.shape), F32)]
-    copies = 1 + 9 + 6 * 9 + 6 * 7 + 2
+    copies = 10 + 6 * 18 + 6 * 9 + 2
     done = wired_call(
         reduce_weights_kernel,
         outs,
@@ -484,7 +535,7 @@
         2,
         "reduce_weights",
         copies,
-        12,
+        6 * 4,
         scratch,
         [ANY] * 5 + [VMEM],
         [ANY] * 7 + [VMEM],

time: 447 us -> 425 us (0.951)
  Pallas kernels: 349 us -> 329 us
    pallas_call x9, Pallas kernels: 292 us -> 253 us  [wired_call(): pl.pallas_call(kernel, out_shape=outs, in_specs=[ANY] * len(ins) if in_sp...]
    pallas_call x1, Pallas kernels: 32.8 us -> 44.1 us  [attend_back(): pl.pallas_call(attend_back_kernel, out_shape=[shape(16, 64, 128), shape(6...]
    pallas_call x1, Pallas kernels: 24.2 us -> 32.8 us  [attend(): pl.pallas_call(attend_kernel, out_shape=[shape(16, 64, 128), shape(16, 12...]
where the time goes in v3:
time: 425 us
  Pallas kernels  329 us (77%)
  local copies, waits for them, and re-layouts  35.2 us (8%)
  matrix products  32.7 us (8%)
  other arithmetic  25.6 us (6%)
    pallas_call x9, Pallas kernels, wired_call(): pl.pallas_call(kernel, out_shape=outs, in_specs=[ANY] * len(ins) if in_sp...  253 us
    pallas_call x1, Pallas kernels, attend_back(): pl.pallas_call(attend_back_kernel, out_shape=[shape(16, 64, 128), shape(6...  44.1 us
    pallas_call x1, Pallas kernels, attend(): pl.pallas_call(attend_kernel, out_shape=[shape(16, 64, 128), shape(16, 12...  32.8 us
    unnamed x196, local copies, waits for them, and re-layouts  20.3 us
    dot_general x10, matrix products, matmul(): return jnp.dot(left, right, preferred_element_type=F32)  17.4 us
    dot_general x5, matrix products, outer_sum(): lax.dot_general(left, right, (((0,), (0,)), ((), ())), preferred_element_...  15.3 us

profile of v3, /device:TPU:0, one launch (start us, length us, event | category | flops | bytes accessed | tf_op | source)
XLA Modules:
  0.0 424.9 jit_solution(10579264113525163600)
XLA Ops:
  0.7 1.7 copy-done.7
  2.3 1.7 copy-done.8
  4.0 1.7 copy-done.9
  7.9 65.0 %gather_weights.1 = (bf16[2,2,4,4,16,2048]{5,4,3,2,1,0:T(8,128)(2,1)S(1)}, bf16[2,2,4,4,16,1024]{5,4,3,2,1,0:T(8,128)(2,1)S(1)}, bf16[2,2,4,4,16,2304]{5,4,3,2,1...) custom-call(bf16[4,4,16,2048]{3,2,1,0:T(8,128)(2,1)S(1)} %bitcast.178, ...), custom_call_target="tpu_custom_call" | custom-call | tf_op jit(solution)/shard_map/gather_weights/pallas_call | solution.py:103
  72.9 2.2 copy-done.28
  81.5 1.8 copy.83
  85.1 1.6 pad_maximum_fusion.2
  92.2 22.9 %to_heads.2 = (bf16[8,128,128]{2,1,0:T(8,128)(2,1)S(1)}, bf16[32,128,128]{2,1,0:T(8,128)(2,1)S(1)}) custom-call(bf16[128,1024]{1,0:T(8,128)(2,1)S(1)} %copy-done.13, bf16[128,1024]{1,0:T(8,128)(2,1)S(1)} %copy.99.refs_1_), custom_call_target="tpu_custom_call" | custom-call | tf_op jit(solution)/shard_map/to_heads/pallas_call | solution.py:103
  116.9 32.8 %attend.1 = (bf16[16,64,128]{2,1,0:T(8,128)(2,1)S(1)}, f32[16,128,128]{2,1,0:T(8,128)S(1)}, f32[16,8,128]{2,1,0:T(8,128)S(1)}) custom-call(s32[64]{0:T(128)S(1)} %copy-done.26, s32[4]{0:T(128)S(1)} %bitcast.189, s32[1]{0:T(128)} %bitcast.2.place_ref, bf16[16,64,128]{2,1,0:T(8,128)(2,1)S(1)} %bitcast.182, bf16[64,64,128]{2,1,0:T(8,128)(2,1)S(1)} %bitcast.170), custom_call_target="tpu_custom_call" | custom-call | tf_op jit(solution)/shard_map/attend/pallas_call | solution.py:807
  150.8 6.6 %to_tokens.2.refs_3_ = bf16[128,1024]{1,0:T(8,128)(2,1)S(1)} custom-call(bf16[8,128,128]{2,1,0:T(8,128)(2,1)S(1)} %bitcast.188), custom_call_target="tpu_custom_call" | custom-call | tf_op jit(solution)/shard_map/to_tokens/pallas_call | solution.py:103
  157.4 1.6 multiply_reduce_fusion.6
  159.9 2.5 share.2
  162.5 1.4 fusion.42
  165.4 2.5 multiply_convert_fusion
  172.3 2.8 hand_over.1
  177.7 2.2 multiply_reduce_fusion.2
  181.8 7.8 %to_heads.3 = bf16[8,128,128]{2,1,0:T(8,128)(2,1)S(1)} custom-call(bf16[128,1024]{1,0:T(8,128)(2,1)S(1)} %convolution_convert_fusion.3.refs_0_), custom_call_target="tpu_custom_call" | custom-call | tf_op jit(solution)/shard_map/to_heads/pallas_call | solution.py:103
  189.7 44.1 %attend_back.1 = (bf16[16,64,128]{2,1,0:T(8,128)(2,1)S(1)}, bf16[64,64,128]{2,1,0:T(8,128)(2,1)S(1)}) custom-call(s32[64]{0:T(128)S(1)} %copy-done.26, s32[4]{0:T(128)S(1)} %bitcast.190, s32[1]{0:T(128)} %bitcast.2.place_ref, bf16[16,64,128]{2,1,0:T(8,128)(2,1)S(1)} %bitcast.183, bf16[64,64,128]{2,1,0:T(8,128)(2,1)S(1)} %bitcast.171, ...), custom_call_target="tpu_custom_call" | custom-call | tf_op jit(solution)/shard_map/attend_back/pallas_call | solution.py:876
  233.8 15.7 %to_tokens.3 = (bf16[128,1024]{1,0:T(8,128)(2,1)S(1)}, bf16[32,128,128]{2,1,0:T(8,128)(2,1)S(1)}) custom-call(bf16[8,128,128]{2,1,0:T(8,128)(2,1)S(1)} %bitcast.187, bf16[32,128,128]{2,1,0:T(8,128)(2,1)S(1)} %bitcast.179), custom_call_target="tpu_custom_call" | custom-call | tf_op jit(solution)/shard_map/to_tokens/pallas_call | solution.py:103
  256.5 4.6 %fusion.11 = (f32[1024]{0:T(1024)S(1)}, f32[128]{0:T(128)S(1)}, f32[128,1024]{1,0:T(8,128)}) fusion(bf16[1,128,1024]{2,1,0:T(8,128)(2,1)S(1)} %copy-done.38, f32[128]{0:T(128)S(1)} %copy-done.86, f32[1024]{0:T(1024)S(1)} %copy-done.74, bf16[1024,2048]{1,0:T(8,128)(2,1)} %bitcast.169, bf16[128,512]{1,0:T(8,128)(2,1)S(1)} %copy.94, ...), kind=kOutput, calls=%fused_computation.39 | convolution fusion | flops 538835840 | bytes 5514240 | tf_op jit(solution)/shard_map/dot_general | solution.py:921
  262.8 2.5 share.3
  265.3 2.4 bitcast_convert_fusion.2
  267.6 2.1 bitcast_convert_fusion
  269.7 3.6 convolution_convert_fusion
  273.3 3.6 convolution_convert_fusion.1
  277.0 3.6 convolution_convert_fusion.2
  280.6 126.8 %reduce_weights.1 = (bf16[2,4,4,16,2304]{4,3,2,1,0:T(8,128)(2,1)}, bf16[2,4,4,16,2304]{4,3,2,1,0:T(8,128)(2,1)}, bf16[4,4,16,2304]{3,2,1,0:T(8,128)(2,1)}, bf16[...) custom-call(bf16[2,2,4,4,16,2304]{5,4,3,2,1,0:T(8,128)(2,1)} %bitcas, ...), custom_call_target="tpu_custom_call" | custom-call | tf_op jit(solution)/shard_map/reduce_weights/pallas_call | solution.py:103
  407.4 1.4 constant_dynamic-slice_fusion.1
  409.5 2.7 maximum_convert_fusion.1
  414.1 2.7 maximum_convert_fusion
  416.8 2.9 bitcast_convert_fusion.1
  419.8 1.6 bitcast_convert_fusion.3
  (265 shorter events, 43.9 us)
Async XLA Ops:
  7.9 67.2 %copy-start.36 = (bf16[1,128,1024]{2,1,0:T(8,128)(2,1)S(1)}, bf16[1,128,1024]{2,1,0:T(8,128)(2,1)}, u32[]{:S(2)}) copy-start(bf16[1,128,1024]{2,1,0:T(8,128)(2,1)} %param.13) | copy-start | bytes 786436
  7.9 68.1 %copy-start.72 = (f32[1024]{0:T(1024)S(1)}, f32[1024]{0:T(1024)}, u32[]{:S(2)}) copy-start(f32[1024]{0:T(1024)} %param.20) | copy-start | bytes 12292
  79.3 8.5 %copy-start.34 = (f32[128,8,64]{2,0,1:T(8,128)}, f32[128,8,64]{2,0,1:T(8,128)S(1)}, u32[]{:S(2)}) copy-start(f32[128,8,64]{2,0,1:T(8,128)S(1)} %copy.79) | copy-start | bytes 786436
  80.5 7.3 %copy-start.57 = (f32[128,32]{1,0:T(8,128)}, f32[128,32]{1,0:T(8,128)S(1)}, u32[]{:S(2)}) copy-start(f32[128,32]{1,0:T(8,128)S(1)} %copy.81) | copy-start | bytes 49156
  81.5 6.3 %slice-start.2 = ((f32[128,2048]{1,0:T(8,128)}), f32[128,1024]{1,0:T(8,128)S(1)}, s32[]{:S(2)}) async-start(f32[128,2048]{1,0:T(8,128)} %copy-done.44), calls=%async_computation.2 | async-start | bytes 1048576 | tf_op jit(solution)/shard_map/jvp()/slice | solution.py:963
  87.8 28.0 %copy-start.27 = (s32[1,4]{1,0:T(1,128)S(1)}, s32[1,4]{1,0:T(1,128)}, u32[]{:S(2)}) copy-start(s32[1,4]{1,0:T(1,128)} %param.25) | copy-start | bytes 52
  115.8 43.3 %copy-start.1 = (bf16[32,128,128]{2,1,0:T(8,128)(2,1)}, bf16[32,128,128]{2,1,0:T(8,128)(2,1)S(1)}, u32[]{:S(2)}) copy-start(bf16[32,128,128]{2,1,0:T(8,128)(2,1)S(1)} %get-tuple-element.43) | copy-start | bytes 3145732
  116.9 42.2 %copy-start.37 = (bf16[1,128,1024]{2,1,0:T(8,128)(2,1)S(1)}, bf16[1,128,1024]{2,1,0:T(8,128)(2,1)}, u32[]{:S(2)}) copy-start(bf16[1,128,1024]{2,1,0:T(8,128)(2,1)} %param.13) | copy-start | bytes 786436
  116.9 42.2 %copy-start.67 = (f32[1024]{0:T(1024)S(1)}, f32[1024]{0:T(1024)}, u32[]{:S(2)}) copy-start(f32[1024]{0:T(1024)} %param.23) | copy-start | bytes 12292
  116.9 42.2 %copy-start.73 = (f32[1024]{0:T(1024)S(1)}, f32[1024]{0:T(1024)}, u32[]{:S(2)}) copy-start(f32[1024]{0:T(1024)} %param.20) | copy-start | bytes 12292
  116.9 42.2 %copy-start.85 = (f32[128]{0:T(128)S(1)}, f32[128]{0:T(128)}, u32[]{:S(2)}) copy-start(f32[128]{0:T(128)} %copy-done.84) | copy-start | bytes 1540
  157.4 5.0 %copy-start.93 = (bf16[2,2,4,4,16,2304]{5,4,3,2,1,0:T(8,128)(2,1)S(1)}, bf16[2,2,4,4,16,2304]{5,4,3,2,1,0:T(8,128)(2,1)}, u32[]{:S(2)}) copy-start(bf16[2,2,4,4,16,2304]{5,4,3,2,1,0:T(8,128)(2,1)} %get-tuple-element.48) | copy-start | bytes 14155780
  159.1 4.8 %copy-start.91 = (f32[128]{0:T(128)}, f32[128]{0:T(128)S(1)}, u32[]{:S(2)}) copy-start(f32[128]{0:T(128)S(1)} %get-tuple-element.111) | copy-start | bytes 1540
  159.1 18.6 %copy-start.78 = (f32[128]{0:T(128)}, f32[128]{0:T(128)S(1)}, u32[]{:S(2)}) copy-start(f32[128]{0:T(128)S(1)} %fusion.33) | copy-start | bytes 1540
  170.9 6.8 %copy-start.68 = (f32[1024]{0:T(1024)S(1)}, f32[1024]{0:T(1024)}, u32[]{:S(2)}) copy-start(f32[1024]{0:T(1024)} %param.23) | copy-start | bytes 12292
  172.3 7.6 %copy-start.92 = (f32[128]{0:T(128)S(1)}, f32[128]{0:T(128)}, u32[]{:S(2)}) copy-start(f32[128]{0:T(128)} %copy-done.91) | copy-start | bytes 1540
  179.9 9.8 %copy-start.42 = (f32[128,1024]{1,0:T(8,128)}, f32[128,1024]{1,0:T(8,128)S(1)}, u32[]{:S(2)}) copy-start(f32[128,1024]{1,0:T(8,128)S(1)} %get-tuple-element.79) | copy-start | bytes 1572868
  179.9 9.8 %copy-start.87 = (f32[128]{0:T(128)}, f32[128]{0:T(128)S(1)}, u32[]{:S(2)}) copy-start(f32[128]{0:T(128)S(1)} %multiply_multiply_fusion.5) | copy-start | bytes 1540
  179.9 9.8 %copy-start.2 = (bf16[32,128,128]{2,1,0:T(8,128)(2,1)S(1)}, bf16[32,128,128]{2,1,0:T(8,128)(2,1)}, u32[]{:S(2)}) copy-start(bf16[32,128,128]{2,1,0:T(8,128)(2,1)} %copy-done.1) | copy-start | bytes 3145732
  179.9 9.8 %copy-start.12 = (f32[16,128,128]{2,1,0:T(8,128)S(1)}, f32[16,128,128]{2,1,0:T(8,128)}, u32[]{:S(2)}) copy-start(f32[16,128,128]{2,1,0:T(8,128)} %copy-done.11) | copy-start | bytes 3145732
  179.9 9.8 %copy-start.16 = (bf16[8,128,128]{2,1,0:T(8,128)(2,1)S(1)}, bf16[8,128,128]{2,1,0:T(8,128)(2,1)}, u32[]{:S(2)}) copy-start(bf16[8,128,128]{2,1,0:T(8,128)(2,1)} %copy-done.14) | copy-start | bytes 786436
  189.7 60.0 %copy-start.58 = (f32[128,32]{1,0:T(8,128)S(1)}, f32[128,32]{1,0:T(8,128)}, u32[]{:S(2)}) copy-start(f32[128,32]{1,0:T(8,128)} %copy-done.57) | copy-start | bytes 49156
  233.8 16.2 %copy-start.35 = (f32[128,8,64]{2,0,1:T(8,128)S(1)}, f32[128,8,64]{2,0,1:T(8,128)}, u32[]{:S(2)}) copy-start(f32[128,8,64]{2,0,1:T(8,128)} %copy-done.34) | copy-start | bytes 786436
  233.8 16.2 %copy-start.71 = (f32[128,8]{0,1:T(8,128)S(1)}, f32[128,8]{0,1:T(8,128)}, u32[]{:S(2)}) copy-start(f32[128,8]{0,1:T(8,128)} %copy-done.70) | copy-start | bytes 12292
  233.8 16.2 %copy-start.82 = (f32[64]{0:T(128)S(1)}, f32[64]{0:T(128)}, u32[]{:S(2)}) copy-start(f32[64]{0:T(128)} %param.22) | copy-start | bytes 772
  256.0 5.0 %copy-start.48 = (bf16[128,1536]{1,0:T(8,128)(2,1)}, bf16[128,1536]{1,0:T(8,128)(2,1)S(1)}, u32[]{:S(2)}) copy-start(bf16[128,1536]{1,0:T(8,128)(2,1)S(1)} %add_convert_fusion) | copy-start | bytes 1179652
  256.5 4.6 %copy-start.77 = (f32[1024]{0:T(1024)S(1)}, f32[1024]{0:T(1024)}, u32[]{:S(2)}) copy-start(f32[1024]{0:T(1024)} %get-tuple-element.73) | copy-start | bytes 12292
  419.7 4.0 copy-start.4
  419.7 4.0 copy-start.19
  419.7 4.0 copy-start.33
  419.7 4.0 copy-start.39
  419.7 4.0 copy-start.43
  (67 other events, 137.1 us)
